TPU v7x, 128 devices: a whole 4x4x4 slice. The times are simulated.
128 devices in a mesh: band: 8 (over z, core), grp: 16 (over x, y).
Axes of the slice: x: 4, y: 4, z: 4, core: 2. Of those that a mesh axis runs over, the one named last changes fastest.
Arguments:
- action: float32 [1296, 65536], P(None, ('band', 'grp')), may hold values from 0.05 to 2
- block_list: int32 [512], P(('band', 'grp')), may hold values from 0 to 63, as said below
- land_sea: int32 [32, 2048], P('band', 'grp'), may hold values from 0 to 1, as said below
- ice: int32 [32, 2048], P('band', 'grp'), may hold values 0 or 1
- depth: float32 [32, 2048], P('band', 'grp'), may hold values from 0.2 to 4
- current_x: float32 [32, 2048], P('band', 'grp'), may hold values from -0.15 to 0.15
- current_y: float32 [32, 2048], P('band', 'grp'), may hold values from -0.15 to 0.15
- wind: float32 [32, 2048], P('band', 'grp'), may hold values from 0.3 to 3
- wind_rate: float32 [1296], replicated, may hold values from 0.05 to 0.5
- dissipation: float32 [1296], replicated, may hold values from 0.05 to 0.5
- mix_first: bfloat16 [1296, 1296], replicated, may hold values from -0.15625 to 0.15625
- mix_second: bfloat16 [1296, 1296], replicated, may hold values from -0.15625 to 0.15625
Outputs:
- spectra: float32 [1296, 65536], P(None, ('band', 'grp'))
Inputs may be any that keep to these rules, and one draw needn't show every extreme that they name: `block_list`: values are block numbers within a sub-band. The lists of the devices of one sub-band (the entries of one run of 64) name each of its blocks once; in each device's run of 4 entries the first 2 name blocks holding at least one sea cell and the others name blocks of land only. `land_sea`: consistent with block_list: blocks of land only are all 0.
All inputs are finite; a program needn't handle non-finite values. No bound on the sum of `ice` on one device may be relied on, other than what follows from the above.
Results may differ from a plain program's by a relative error of at most 0.0016.
Values may be sent and summed in bfloat16 or wider, within the bound.
A program may use at most 128 MiB of HBM per device.

v0:
```python
import functools
import math

import jax
import jax.numpy as jnp
import numpy as np
from jax import lax
from jax.experimental import pallas as pl
from jax.experimental.pallas import tpu as pltpu
from jax.sharding import PartitionSpec as P

ND = 36
K = 1296
TILE = 16
TILES = 81
BLK = 128
MEM = 16
BANDS = 8
SLOTS = 32
STEPS = 2
CHUNKS = 5
EXTRA = 5
HOT = 0
ZERO = 32
HALO = 33
FIELD = 49
MESH = pl.DeviceIdType.MESH
F32 = jnp.float32
BF16 = jnp.bfloat16


def component_table():
    index = np.arange(K)
    freq = (index // ND).astype(np.float64)
    angle = 2.0 * math.pi * (index % ND) / ND
    table = np.zeros((K, BLK), np.float32)
    table[:, 0] = 1.0 + 0.25 * freq
    table[:, 1] = 0.4 * 0.93**freq
    table[:, 2] = np.cos(angle)
    table[:, 3] = np.sin(angle)
    return table.reshape(TILES, TILE, BLK)


def kernel(
    bl, land, ice, depth, cur_x, cur_y, wind, wr, dis, cst, action, mix1, mix2,
    out,
    S, M1, M2, LOW, F1, F2, G, A, R, D, HO, HI, FE, FW, FN, FS, VX, VY, SM,
    MT, META, IDT, IDS, TBL, TBS, NB, C, WRB, DSB, OW, ACC,
    act_sem, mix_sem, cst_sem, tbl_sem, meta_send, meta_recv, id_send, id_recv,
    out_send, out_recv, halo_send, halo_recv, ret_send, ret_recv, fin_sem,
):
    band = lax.axis_index("band")
    me = lax.axis_index("grp")
    mx, my = me // 4, me % 4
    up, down = (band + 1) % BANDS, (band + BANDS - 1) % BANDS

    def peer(o):
        return ((mx + o // 4) % 4) * 4 + (my + o % 4) % 4

    def rows_of(t):
        return (1280, 16) if t == EXTRA else (256 * t, 256)

    order = [EXTRA] + list(range(CHUNKS))

    loads = {}
    for t in order:
        r0, n = rows_of(t)
        loads[t] = pltpu.make_async_copy(
            action.at[pl.ds(r0, n), pl.ds(0, 256)], S.at[pl.ds(r0, n)], act_sem.at[t]
        )
        loads[t].start()
    table_loads = []
    for t in range(CHUNKS + 1):
        tile = 80 if t == EXTRA else 16 * t + me
        table_loads.append(pltpu.make_async_copy(cst.at[tile], C.at[t], cst_sem.at[t]))
        table_loads[-1].start()
    mix_loads = [
        pltpu.make_async_copy(mix1, M1, mix_sem.at[0]),
        pltpu.make_async_copy(mix2, M2, mix_sem.at[1]),
    ]
    for one in mix_loads:
        one.start()

    barrier = pltpu.get_barrier_semaphore()

    def greet(o, carry):
        pl.semaphore_signal(barrier, inc=1, device_id=(band, peer(o)), device_id_type=MESH)
        return carry

    lax.fori_loop(1, MEM, greet, 0)
    pl.semaphore_signal(barrier, inc=1, device_id=(up, me), device_id_type=MESH)
    pl.semaphore_signal(barrier, inc=1, device_id=(down, me), device_id_type=MESH)

    wet = land[...].astype(F32) * (1.0 - ice[...].astype(F32))
    MT[0:4] = wet * depth[...]
    MT[4:8] = wet * cur_x[...]
    MT[8:12] = wet * cur_y[...]
    MT[12:16] = wind[...]
    IDT[...] = jnp.zeros_like(IDT)
    IDT[0:1] = jnp.full((1, BLK), bl[0], jnp.int32)
    IDT[1:2] = jnp.full((1, BLK), bl[1], jnp.int32)
    META[me] = MT[...]
    IDS[me] = IDT[...]
    for ref in (FE, FW, FN, FS):
        for par in range(2):
            ref[par, ZERO] = jnp.zeros((TILE, BLK), F32)

    pl.semaphore_wait(barrier, MEM + 1)

    def send_meta(o, carry):
        dst = peer(o)
        pltpu.make_async_remote_copy(
            src_ref=IDT, dst_ref=IDS.at[me], send_sem=id_send, recv_sem=id_recv,
            device_id=(band, dst), device_id_type=MESH,
        ).start()
        pltpu.make_async_remote_copy(
            src_ref=MT, dst_ref=META.at[me], send_sem=meta_send, recv_sem=meta_recv,
            device_id=(band, dst), device_id_type=MESH,
        ).start()
        return carry

    lax.fori_loop(1, MEM, send_meta, 0)

    def send_out(s, t):
        if t == EXTRA:
            @pl.when(me != HOT)
            def _():
                pltpu.make_async_remote_copy(
                    src_ref=G.at[s, 80], dst_ref=A.at[s, EXTRA, me],
                    send_sem=out_send.at[s, 1], recv_sem=out_recv.at[s, EXTRA],
                    device_id=(band, HOT), device_id_type=MESH,
                ).start()

            @pl.when(me == HOT)
            def _():
                A[s, EXTRA, HOT] = G[s, 80]
            return

        def one(o, carry):
            dst = peer(o)
            pltpu.make_async_remote_copy(
                src_ref=G.at[s, 16 * t + dst], dst_ref=A.at[s, t, me],
                send_sem=out_send.at[s, 0], recv_sem=out_recv.at[s, t],
                device_id=(band, dst), device_id_type=MESH,
            ).start()
            return carry

        lax.fori_loop(1, MEM, one, 0)
        A[s, t, me] = G[s, 16 * t + me]

    for t in order:
        r0, n = rows_of(t)
        loads[t].wait()

        def pack(i, carry, r0=r0):
            rows = pl.ds(pl.multiple_of(r0 + i * TILE, TILE), TILE)
            for sl in range(2):
                G[0, r0 // TILE + i, sl] = S[rows, sl * BLK:(sl + 1) * BLK].astype(BF16)
            return carry

        lax.fori_loop(0, n // TILE, pack, 0)
        send_out(0, t)

    def columns(i, carry):
        part = pl.ds(pl.multiple_of(i * BLK, BLK), BLK)
        diag = lax.broadcasted_iota(jnp.int32, (BLK, BLK), 0) == lax.broadcasted_iota(jnp.int32, (BLK, BLK), 1)
        for src, dst in ((wr, WRB), (dis, DSB)):
            col = jnp.sum(jnp.where(diag, src[0:1, part], 0.0), axis=1, keepdims=True)
            dst[part, :] = jnp.broadcast_to(col, (BLK, BLK))
        return carry

    lax.fori_loop(0, K // BLK, columns, 0)
    rest = K % BLK
    diag = lax.broadcasted_iota(jnp.int32, (rest, rest), 0) == lax.broadcasted_iota(jnp.int32, (rest, rest), 1)
    for src, dst in ((wr, WRB), (dis, DSB)):
        col = jnp.sum(jnp.where(diag, src[0:1, K - rest:K], 0.0), axis=1, keepdims=True)
        dst[K - rest:K, :] = jnp.broadcast_to(col, (rest, BLK))

    def wait_for(ref, sem):
        pltpu.make_async_copy(ref, ref, sem).wait()

    wait_for(IDS.at[pl.ds(0, MEM - 1)], id_recv)
    lane = lax.broadcasted_iota(jnp.int32, (1, BLK), 1)
    inverse = jnp.full((1, BLK), ZERO, jnp.int32)
    named = jnp.zeros((1, BLK), jnp.int32)
    for i in range(MEM):
        for sl in range(2):
            j = 2 * i + sl
            ident = IDS[i, sl:sl + 1, :]
            inverse = jnp.where(lane == ident + 16, j, inverse)
            named = jnp.where(lane == j, ident, named)
    inverse = jnp.where(lane < 16, HALO + lane, inverse)
    inverse = jnp.where(jnp.logical_and(lane >= 80, lane < 96), HALO + lane - 80, inverse)
    TBL[...] = jnp.zeros_like(TBL)
    TBL[0:1] = inverse
    TBL[1:2] = named
    to_smem = pltpu.make_async_copy(TBL, TBS, tbl_sem)
    to_smem.start()
    to_smem.wait()

    def neighbours(j, carry):
        q = TBS[1, j]
        line, place = (q // 16) * 16 + 16, q % 16
        NB[0, j] = TBS[0, line + (place + 15) % 16]
        NB[1, j] = TBS[0, line + (place + 1) % 16]
        NB[2, j] = TBS[0, q]
        NB[3, j] = TBS[0, q + 32]
        return carry

    lax.fori_loop(0, SLOTS, neighbours, 0)

    wait_for(META.at[pl.ds(0, MEM - 1)], meta_recv)

    def at_block(q):
        found = META[q % 16]
        r = q // 16
        pick = []
        for layer in range(4):
            got = found[4 * layer:4 * layer + 1]
            for k in range(1, 4):
                got = jnp.where(r == k, found[4 * layer + k:4 * layer + k + 1], got)
            pick.append(got)
        return pick

    def place_meta(j, carry):
        wd, wx, wy, _ = at_block(TBS[1, j])
        SM[j, 0:1] = wd
        SM[j, 1:2] = wx
        SM[j, 2:3] = wy
        SM[j, 3:4] = jnp.where(wd > 0.0, 1.0, 0.0)
        return carry

    lax.fori_loop(0, SLOTS, place_meta, 0)
    for sl in range(2):
        wd, _, _, wn = at_block(bl[sl])
        OW[0:1, sl * BLK:(sl + 1) * BLK] = jnp.where(wd > 0.0, 1.0, 0.0)
        OW[1:2, sl * BLK:(sl + 1) * BLK] = wn
    for one in table_loads:
        one.wait()

    lanes = lax.broadcasted_iota(jnp.int32, (TILE, BLK), 1)
    below = jnp.where(band > 0, 1.0, 0.0)
    above = jnp.where(band < BANDS - 1, 1.0, 0.0)

    def halo_copy(s, t, way):
        return pltpu.make_async_remote_copy(
            src_ref=HO.at[s, t, way], dst_ref=HI.at[s, t, way],
            send_sem=halo_send.at[s, t, way], recv_sem=halo_recv.at[s, t, way],
            device_id=(up if way == 0 else down, me), device_id_type=MESH,
        )

    def fluxes(s, t, par):
        count = MEM - 1
        wait_for(A.at[s, t, pl.ds(0, count)], out_recv.at[s, t])
        consts = C[t]
        aa, bb, cc, ss = (jnp.broadcast_to(consts[:, i:i + 1], (TILE, BLK)) for i in range(4))

        def one(i, carry):
            for sl in range(2):
                j = 2 * i + sl
                g = A[s, t, i, sl].astype(F32)
                if s == 0:
                    here = SM[j]
                    speed = bb * jnp.tanh(aa * here[0:1])
                    vx = speed * cc + here[1:2]
                    vy = speed * ss + here[2:3]
                    VX[t, j] = vx
                    VY[t, j] = vy
                else:
                    vx = VX[t, j]
                    vy = VY[t, j]
                px = vx * g
                east = jnp.where(vx > 0.0, px, 0.0)
                FE[par, j] = east
                FW[par, j] = east - px
                py = vy * g
                north = jnp.where(vy > 0.0, py, 0.0)
                FN[par, j] = north
                FS[par, j] = north - py
            return carry

        lax.fori_loop(0, MEM, one, 0, unroll=2)

        def edge(p, carry):
            HO[s, t, 0, p] = FN[par, TBS[0, 64 + p]].astype(BF16)
            HO[s, t, 1, p] = FS[par, TBS[0, 16 + p]].astype(BF16)
            return carry

        lax.fori_loop(0, MEM, edge, 0, unroll=2)
        halo_copy(s, t, 0).start()
        halo_copy(s, t, 1).start()

    def changes(s, t, par):
        halo_copy(s, t, 0).wait_recv()
        halo_copy(s, t, 1).wait_recv()

        def edge(p, carry):
            FN[par, HALO + p] = HI[s, t, 0, p].astype(F32) * below
            FS[par, HALO + p] = HI[s, t, 1, p].astype(F32) * above
            return carry

        lax.fori_loop(0, MEM, edge, 0, unroll=2)

        def one(i, carry):
            for sl in range(2):
                j = 2 * i + sl
                east, west = FE[par, j], FW[par, j]
                leaving = east + west + FN[par, j] + FS[par, j]
                come = FN[par, NB[2, j]] + FS[par, NB[3, j]]
                come += pltpu.roll(jnp.where(lanes == BLK - 1, FE[par, NB[0, j]], east), 1, 1)
                come += pltpu.roll(jnp.where(lanes == 0, FW[par, NB[1, j]], west), BLK - 1, 1)
                R[s, t, i, sl] = (SM[j, 3:4] * (come - leaving)).astype(BF16)
            return carry

        lax.fori_loop(0, MEM, one, 0, unroll=2)
        tile = 80 if t == EXTRA else 16 * t + me

        def send(o, carry):
            dst = peer(o)
            pltpu.make_async_remote_copy(
                src_ref=R.at[s, t, dst], dst_ref=D.at[s, tile],
                send_sem=ret_send.at[s, 1 if t == EXTRA else 0], recv_sem=ret_recv.at[s, t],
                device_id=(band, dst), device_id_type=MESH,
            ).start()
            return carry

        lax.fori_loop(1, MEM, send, 0)
        D[s, tile] = R[s, t, me]

    def combine(s, t):
        r0, n = rows_of(t)
        if t == EXTRA:
            @pl.when(me != HOT)
            def _():
                wait_for(D.at[s, 80], ret_recv.at[s, EXTRA])
        else:
            wait_for(D.at[s, pl.ds(16 * t, MEM - 1)], ret_recv.at[s, t])

        def one(i, carry):
            rows = pl.ds(pl.multiple_of(r0 + i * TILE, TILE), TILE)
            sums = []
            for sl in range(2):
                cols = slice(sl * BLK, (sl + 1) * BLK)
                x = S[rows, cols]
                if s == 0:
                    x = x * OW[0:1, cols]
                x = x + D[s, r0 // TILE + i, sl].astype(F32)
                S[rows, cols] = x
                LOW[rows, cols] = x.astype(BF16)
                sums.append(carry[sl] + x * x)
            return tuple(sums)

        got = lax.fori_loop(0, n // TILE, one, (ACC[0], ACC[1]), unroll=2 if n > TILE else 1)
        ACC[0], ACC[1] = got

    def source(s, t, spread):
        r0, n = rows_of(t)
        low = LOW[...]
        F1[0:n] = jnp.dot(M1[r0:r0 + n, :], low, preferred_element_type=F32)
        F2[0:n] = jnp.dot(M2[r0:r0 + n, :], low, preferred_element_type=F32)

        def one(i, carry):
            rows = pl.ds(pl.multiple_of(r0 + i * TILE, TILE), TILE)
            part = pl.ds(pl.multiple_of(i * TILE, TILE), TILE)
            for sl in range(2):
                cols = slice(sl * BLK, (sl + 1) * BLK)
                x = S[rows, cols]
                scale = 1.0 + 0.5 * (WRB[rows, :] * OW[1:2, cols] - DSB[rows, :] * spread[sl])
                x = OW[0:1, cols] * (x * scale + 0.25 * F1[part, cols] * (1.0 + jnp.tanh(0.5 * F2[part, cols])))
                S[rows, cols] = x
                if s == 0:
                    G[1, r0 // TILE + i, sl] = x.astype(BF16)
            return carry

        lax.fori_loop(0, n // TILE, one, 0, unroll=2 if n > TILE else 1)

    def result_copy(t):
        r0, n = rows_of(t)
        return pltpu.make_async_copy(S.at[pl.ds(r0, n)], out.at[pl.ds(r0, n)], fin_sem.at[t])

    for s in range(STEPS):
        @pl.when(me == HOT)
        def _():
            fluxes(s, EXTRA, 0)
        for t in range(CHUNKS):
            fluxes(s, t, (t + 1) % 2)
            if t == 0:
                @pl.when(me == HOT)
                def _():
                    changes(s, EXTRA, 0)
            else:
                changes(s, t - 1, t % 2)
        changes(s, CHUNKS - 1, CHUNKS % 2)

        ACC[...] = jnp.zeros_like(ACC)
        for t in order:
            combine(s, t)
        spread = [
            jnp.sqrt(jnp.sum(ACC[sl], axis=0, keepdims=True) * (1.0 / K) + 1e-06) for sl in range(2)
        ]
        if s == 0:
            for one in mix_loads:
                one.wait()
        for t in order:
            source(s, t, spread)
            if s == 0:
                send_out(1, t)
            else:
                result_copy(t).start()

    wait_for(IDS.at[pl.ds(0, MEM - 1)], id_send)
    wait_for(META.at[pl.ds(0, MEM - 1)], meta_send)
    for s in range(STEPS):
        wait_for(G.at[s, pl.ds(0, 75)], out_send.at[s, 0])
        wait_for(D.at[s, pl.ds(0, 75)], ret_send.at[s, 0])

        @pl.when(me != HOT)
        def _():
            wait_for(G.at[s, 80], out_send.at[s, 1])

        @pl.when(me == HOT)
        def _():
            wait_for(R.at[s, EXTRA, pl.ds(0, MEM - 1)], ret_send.at[s, 1])
            for way in range(2):
                halo_copy(s, EXTRA, way).wait_send()
        for t in range(CHUNKS):
            for way in range(2):
                halo_copy(s, t, way).wait_send()
    for t in order:
        result_copy(t).wait()


def on_device(action, block_list, land_sea, ice, depth, cur_x, cur_y, wind, wind_rate, dissipation, mix1, mix2):
    vmem = pl.BlockSpec(memory_space=pltpu.VMEM)
    hbm = pl.BlockSpec(memory_space=pl.ANY)
    smem = pl.BlockSpec(memory_space=pltpu.SMEM)
    dma = pltpu.SemaphoreType.DMA
    tile = (TILE, BLK)
    wet_part = pl.pallas_call(
        kernel,
        out_shape=jax.ShapeDtypeStruct((K, 256), F32),
        in_specs=[smem] + [vmem] * 8 + [hbm] * 4,
        out_specs=hbm,
        scratch_shapes=[
            pltpu.VMEM((K, 256), F32),
            pltpu.VMEM((K, K), BF16),
            pltpu.VMEM((K, K), BF16),
            pltpu.VMEM((K, 256), BF16),
            pltpu.VMEM((256, 256), F32),
            pltpu.VMEM((256, 256), F32),
            pltpu.VMEM((STEPS, TILES, 2) + tile, BF16),
            pltpu.VMEM((STEPS, 6, MEM, 2) + tile, BF16),
            pltpu.VMEM((STEPS, 6, MEM, 2) + tile, BF16),
            pltpu.VMEM((STEPS, TILES, 2) + tile, BF16),
            pltpu.VMEM((STEPS, 6, 2, MEM) + tile, BF16),
            pltpu.VMEM((STEPS, 6, 2, MEM) + tile, BF16),
            pltpu.VMEM((2, FIELD) + tile, F32),
            pltpu.VMEM((2, FIELD) + tile, F32),
            pltpu.VMEM((2, FIELD) + tile, F32),
            pltpu.VMEM((2, FIELD) + tile, F32),
            pltpu.VMEM((6, SLOTS) + tile, F32),
            pltpu.VMEM((6, SLOTS) + tile, F32),
            pltpu.VMEM((SLOTS, 8, BLK), F32),
            pltpu.VMEM((16, BLK), F32),
            pltpu.VMEM((MEM, 16, BLK), F32),
            pltpu.VMEM((8, BLK), jnp.int32),
            pltpu.VMEM((MEM, 8, BLK), jnp.int32),
            pltpu.VMEM((8, BLK), jnp.int32),
            pltpu.SMEM((8, BLK), jnp.int32),
            pltpu.SMEM((4, SLOTS), jnp.int32),
            pltpu.VMEM((6,) + tile, F32),
            pltpu.VMEM((K, BLK), F32),
            pltpu.VMEM((K, BLK), F32),
            pltpu.VMEM((8, 256), F32),
            pltpu.VMEM((2,) + tile, F32),
            dma((6,)), dma((2,)), dma((6,)), dma, dma, dma, dma, dma,
            dma((STEPS, 2)), dma((STEPS, 6)), dma((STEPS, 6, 2)), dma((STEPS, 6, 2)),
            dma((STEPS, 2)), dma((STEPS, 6)), dma((6,)),
        ],
        compiler_params=pltpu.CompilerParams(
            collective_id=0, has_side_effects=True, vmem_limit_bytes=48 * 1024 * 1024
        ),
        cost_estimate=pl.CostEstimate(flops=7 * 10**9, bytes_accessed=10**7, transcendentals=10**6),
    )(
        block_list, land_sea, ice, depth, cur_x, cur_y, wind,
        wind_rate.reshape(1, K), dissipation.reshape(1, K),
        jnp.asarray(component_table()), action, mix1, mix2,
    )
    return jnp.concatenate([wet_part, jnp.zeros((K, action.shape[1] - 256), F32)], axis=1)


def solution(mesh):
    col = P(None, ("band", "grp"))
    flat = P(("band", "grp"))
    grid = P("band", "grp")
    return jax.shard_map(
        on_device,
        mesh=mesh,
        in_specs=(col, flat, grid, grid, grid, grid, grid, grid, P(), P(), P(), P()),
        out_specs=col,
        check_vma=False,
    )
```

profile of v0, /device:TPU:0, one launch (start us, length us, event | category | flops | bytes accessed | tf_op | source)
XLA Modules:
  0.0 80.2 jit_solution(17411915003656454974)
XLA Ops:
  0.0 0.7 reshape.6.wr
  0.7 0.7 reshape.7.dis
  1.4 0.0 copy-start
  1.4 1.7 %copy-done = f32[1296,512]{1,0:T(8,128)S(1)} copy-done((f32[1296,512]{1,0:T(8,128)S(1)}, f32[1296,512]{1,0:T(8,128)}, u32[]{:S(2)}) %copy-start) | copy-done | bytes 2654232
  3.2 0.0 copy-start.1
  3.2 0.7 copy-done.1
  3.8 0.0 copy-start.2
  3.8 0.7 copy-done.2
  4.5 0.0 copy-start.3
  4.5 0.7 copy-done.3
  5.2 0.0 copy-start.4
  5.2 0.7 copy-done.4
  5.9 0.0 copy-start.5
  5.9 0.7 copy-done.5
  6.6 0.0 copy-start.6
  6.6 0.7 copy-done.6
  7.2 0.0 copy-start.7
  7.2 0.7 copy-done.7
  7.9 0.0 copy-start.8
  7.9 1.1 %copy-done.8 = f32[81,16,128]{2,1,0:T(8,128)S(1)} copy-done((f32[81,16,128]{2,1,0:T(8,128)S(1)}, f32[81,16,128]{2,1,0:T(8,128)}, u32[]{:S(2)}) %copy-start.8) | copy-done | bytes 663576
  9.0 69.4 %shard_map.127 = f32[1296,256]{1,0:T(8,128)S(1)} custom-call(s32[4]{0:T(128)S(1)} %copy-done.7, s32[4,128]{1,0:T(4,128)S(1)} %copy-done.1, s32[4,128]{1,0:T(4,128)S(1)} %copy-done.2, f32[4,128]{1,0:T(4,128)S(1)} %copy-done.3, f32[4,128]{1,0:T(4,128)S(1)} %copy-done.4, f32[4,128]{1,0:T(4,128)S(1)} %copy-done.5, f32[4,128]{1,0:T(4,128)S(1)} %copy-done.6, ...), custom_call_target="tpu_custom_call" | custom-call | flops 7000000000 | bytes 10000000 | tf_op jit(solution)/shard_map/pallas_call | solution.py:439
  78.4 1.8 %concatenate.3 = f32[1296,512]{1,0:T(8,128)} pad(f32[1296,256]{1,0:T(8,128)S(1)} %shard_map.127, f32[]{:T(128)} %constant.1.clone.1), padding=0_0x0_256 | pad | bytes 3981316 | tf_op jit(solution)/shard_map/concatenate | solution.py:489
Async XLA Ops:
  1.4 1.7 %copy-start = (f32[1296,512]{1,0:T(8,128)S(1)}, f32[1296,512]{1,0:T(8,128)}, u32[]{:S(2)}) copy-start(f32[1296,512]{1,0:T(8,128)} %action.1) | copy-start | bytes 7962628
  3.2 0.7 copy-start.1
  3.8 0.7 copy-start.2
  4.5 0.7 copy-start.3
  5.2 0.7 copy-start.4
  5.9 0.7 copy-start.5
  6.6 0.7 copy-start.6
  7.2 0.7 copy-start.7
  7.9 1.1 %copy-start.8 = (f32[81,16,128]{2,1,0:T(8,128)S(1)}, f32[81,16,128]{2,1,0:T(8,128)}, u32[]{:S(2)}) copy-start(f32[81,16,128]{2,1,0:T(8,128)} %constant.4.clone.cst) | copy-start | bytes 1990660
where the time goes:
time: 80.7 us; the launch traced here: 80.2 us
  Pallas kernels  69.4 us (86%)
  local copies, waits for them, and re-layouts  10.8 us (13%)
    pallas_call x1, Pallas kernels, on_device(): pl.pallas_call(kernel, out_shape=jax.ShapeDtypeStruct((K, 256), F32), in_...  69.4 us
    unnamed x18, local copies, waits for them, and re-layouts  7.58 us
    concatenate x1, local copies, waits for them, and re-layouts, on_device(): jnp.concatenate([wet_part, jnp.zeros((K, action.shape[1] - 256), F32)], a...  1.85 us

commit v1 on v0

v1 whole, which is shorter than its diff:
```python
import functools
import math

import jax
import jax.numpy as jnp
import numpy as np
from jax import lax
from jax.experimental import pallas as pl
from jax.experimental.pallas import tpu as pltpu
from jax.sharding import PartitionSpec as P

ND = 36
K = 1296
TILE = 16
TILES = 81
BLK = 128
MEM = 16
BANDS = 8
SLOTS = 32
STEPS = 2
CHUNKS = 5
EXTRA = 5
HOT = 0
ZERO = 32
HALO = 33
FIELD = 49
MESH = pl.DeviceIdType.MESH
F32 = jnp.float32
BF16 = jnp.bfloat16


def component_table():
    index = np.arange(K)
    freq = (index // ND).astype(np.float64)
    angle = 2.0 * math.pi * (index % ND) / ND
    table = np.zeros((K, BLK), np.float32)
    table[:, 0] = 1.0 + 0.25 * freq
    table[:, 1] = 0.4 * 0.93**freq
    table[:, 2] = np.cos(angle)
    table[:, 3] = np.sin(angle)
    return table.reshape(TILES, TILE, BLK)


def kernel(
    bl_in, land_in, ice_in, depth_in, cur_x_in, cur_y_in, wind_in, wr_in, dis_in, cst, action, mix1, mix2,
    out,
    bl, land, ice, depth, cur_x, cur_y, wind, wr, dis,
    S, M1, M2, LOW, F1, F2, G, A, R, D, HO, HI, NET, EDGE, FN, FS, VX, VY, SM,
    MT, META, IDT, IDS, TBL, TBS, NB, C, WRB, DSB, OW,
    small_sem, act_sem, mix_sem, cst_sem, tbl_sem, meta_send, meta_recv, id_send, id_recv,
    out_send, out_recv, halo_send, halo_recv, ret_send, ret_recv,
):
    band = lax.axis_index("band")
    me = lax.axis_index("grp")
    mx, my = me // 4, me % 4
    up, down = (band + 1) % BANDS, (band + BANDS - 1) % BANDS

    def peer(o):
        return ((mx + o // 4) % 4) * 4 + (my + o % 4) % 4

    def rows_of(t):
        return (1280, 16) if t == EXTRA else (256 * t, 256)

    order = [EXTRA] + list(range(CHUNKS))

    smalls = (
        (land_in, land), (ice_in, ice), (depth_in, depth), (cur_x_in, cur_x), (cur_y_in, cur_y),
        (wind_in, wind), (bl_in, bl), (wr_in, wr), (dis_in, dis),
    )
    small_loads = [pltpu.make_async_copy(a, c, small_sem.at[i]) for i, (a, c) in enumerate(smalls)]
    for one in small_loads:
        one.start()
    loads = {}
    for t in order:
        r0, n = rows_of(t)
        loads[t] = pltpu.make_async_copy(
            action.at[pl.ds(r0, n), pl.ds(0, 256)], S.at[pl.ds(r0, n)], act_sem.at[t]
        )
        loads[t].start()
    table_loads = []
    for t in range(CHUNKS + 1):
        tile = 80 if t == EXTRA else 16 * t + me
        table_loads.append(pltpu.make_async_copy(cst.at[tile], C.at[t], cst_sem.at[t]))
        table_loads[-1].start()
    mix_loads = [
        pltpu.make_async_copy(mix1, M1, mix_sem.at[0]),
        pltpu.make_async_copy(mix2, M2, mix_sem.at[1]),
    ]
    for one in mix_loads:
        one.start()

    barrier = pltpu.get_barrier_semaphore()

    def greet(o, carry):
        pl.semaphore_signal(barrier, inc=1, device_id=(band, peer(o)), device_id_type=MESH)
        return carry

    lax.fori_loop(1, MEM, greet, 0)
    pl.semaphore_signal(barrier, inc=1, device_id=(up, me), device_id_type=MESH)
    pl.semaphore_signal(barrier, inc=1, device_id=(down, me), device_id_type=MESH)

    for one in small_loads[:7]:
        one.wait()
    wet = land[...].astype(F32) * (1.0 - ice[...].astype(F32))
    MT[0:4] = wet * depth[...]
    MT[4:8] = wet * cur_x[...]
    MT[8:12] = wet * cur_y[...]
    MT[12:16] = wind[...]
    IDT[...] = jnp.zeros_like(IDT)
    IDT[0:1] = jnp.full((1, BLK), bl[0], jnp.int32)
    IDT[1:2] = jnp.full((1, BLK), bl[1], jnp.int32)
    META[me] = MT[...]
    IDS[me] = IDT[...]
    for ref in (EDGE, FN, FS):
        for par in range(2):
            ref[par, ZERO] = jnp.zeros((TILE, BLK), ref.dtype)

    pl.semaphore_wait(barrier, MEM + 1)

    def send_meta(o, carry):
        dst = peer(o)
        pltpu.make_async_remote_copy(
            src_ref=IDT, dst_ref=IDS.at[me], send_sem=id_send, recv_sem=id_recv,
            device_id=(band, dst), device_id_type=MESH,
        ).start()
        pltpu.make_async_remote_copy(
            src_ref=MT, dst_ref=META.at[me], send_sem=meta_send, recv_sem=meta_recv,
            device_id=(band, dst), device_id_type=MESH,
        ).start()
        return carry

    lax.fori_loop(1, MEM, send_meta, 0)

    def send_out(s, t):
        if t is EXTRA:
            @pl.when(me != HOT)
            def _():
                pltpu.make_async_remote_copy(
                    src_ref=G.at[s, 80], dst_ref=A.at[s, EXTRA, me],
                    send_sem=out_send.at[s, 1], recv_sem=out_recv.at[s, EXTRA],
                    device_id=(band, HOT), device_id_type=MESH,
                ).start()

            @pl.when(me == HOT)
            def _():
                A[s, EXTRA, HOT] = G[s, 80]
            return

        def one(o, carry):
            dst = peer(o)
            pltpu.make_async_remote_copy(
                src_ref=G.at[s, 16 * t + dst], dst_ref=A.at[s, t, me],
                send_sem=out_send.at[s, 0], recv_sem=out_recv.at[s, t],
                device_id=(band, dst), device_id_type=MESH,
            ).start()
            return carry

        lax.fori_loop(1, MEM, one, 0)
        A[s, t, me] = G[s, 16 * t + me]

    for t in order:
        r0, n = rows_of(t)
        loads[t].wait()

        def pack(i, carry, r0=r0):
            rows = pl.ds(pl.multiple_of(r0 + i * TILE, TILE), TILE)
            for sl in range(2):
                G[0, r0 // TILE + i, sl] = S[rows, sl * BLK:(sl + 1) * BLK].astype(BF16)
            return carry

        lax.fori_loop(0, n // TILE, pack, 0)
        send_out(0, t)

    for one in small_loads[7:]:
        one.wait()

    def columns(i, carry):
        part = pl.ds(pl.multiple_of(i * BLK, BLK), BLK)
        diag = lax.broadcasted_iota(jnp.int32, (BLK, BLK), 0) == lax.broadcasted_iota(jnp.int32, (BLK, BLK), 1)
        for src, dst in ((wr, WRB), (dis, DSB)):
            col = jnp.sum(jnp.where(diag, src[part].reshape(1, BLK), 0.0), axis=1, keepdims=True)
            dst[part, :] = jnp.broadcast_to(col, (BLK, BLK))
        return carry

    lax.fori_loop(0, K // BLK, columns, 0)
    rest = K % BLK
    diag = lax.broadcasted_iota(jnp.int32, (rest, rest), 0) == lax.broadcasted_iota(jnp.int32, (rest, rest), 1)
    for src, dst in ((wr, WRB), (dis, DSB)):
        col = jnp.sum(jnp.where(diag, src[K - rest:K].reshape(1, rest), 0.0), axis=1, keepdims=True)
        dst[K - rest:K, :] = jnp.broadcast_to(col, (rest, BLK))

    def wait_for(ref, sem):
        pltpu.make_async_copy(ref, ref, sem).wait()

    wait_for(IDS.at[pl.ds(0, MEM - 1)], id_recv)
    lane = lax.broadcasted_iota(jnp.int32, (1, BLK), 1)
    inverse = jnp.full((1, BLK), ZERO, jnp.int32)
    named = jnp.zeros((1, BLK), jnp.int32)
    for i in range(MEM):
        for sl in range(2):
            j = 2 * i + sl
            ident = IDS[i, sl:sl + 1, :]
            inverse = jnp.where(lane == ident + 16, j, inverse)
            named = jnp.where(lane == j, ident, named)
    inverse = jnp.where(lane < 16, jnp.where(band > 0, HALO + lane, ZERO), inverse)
    rim = jnp.where(band < BANDS - 1, HALO + lane - 80, ZERO)
    inverse = jnp.where(jnp.logical_and(lane >= 80, lane < 96), rim, inverse)
    TBL[...] = jnp.zeros_like(TBL)
    TBL[0:1] = inverse
    TBL[1:2] = named
    to_smem = pltpu.make_async_copy(TBL, TBS, tbl_sem)
    to_smem.start()
    to_smem.wait()

    def neighbours(j, carry):
        q = TBS[1, j]
        line, place = (q // 16) * 16 + 16, q % 16
        NB[0, j] = TBS[0, line + (place + 15) % 16]
        NB[1, j] = TBS[0, line + (place + 1) % 16]
        NB[2, j] = TBS[0, q]
        NB[3, j] = TBS[0, q + 32]
        return carry

    lax.fori_loop(0, SLOTS, neighbours, 0)

    wait_for(META.at[pl.ds(0, MEM - 1)], meta_recv)

    def at_block(q):
        found = META[q % 16]
        r = q // 16
        pick = []
        for layer in range(4):
            got = found[4 * layer:4 * layer + 1]
            for k in range(1, 4):
                got = jnp.where(r == k, found[4 * layer + k:4 * layer + k + 1], got)
            pick.append(got)
        return pick

    def place_meta(j, carry):
        wd, wx, wy, _ = at_block(TBS[1, j])
        SM[j, 0:1] = wd
        SM[j, 1:2] = wx
        SM[j, 2:3] = wy
        return carry

    lax.fori_loop(0, SLOTS, place_meta, 0)
    for sl in range(2):
        wd, _, _, wn = at_block(bl[sl])
        OW[0:1, sl * BLK:(sl + 1) * BLK] = jnp.where(wd > 0.0, 1.0, 0.0)
        OW[1:2, sl * BLK:(sl + 1) * BLK] = 0.5 * wn
    for one in table_loads:
        one.wait()

    lanes = lax.broadcasted_iota(jnp.int32, (TILE, BLK), 1)
    first_lane, last_lane = lanes == 0, lanes == BLK - 1

    def halo_copy(s, c, way):
        return pltpu.make_async_remote_copy(
            src_ref=HO.at[s, c, way], dst_ref=HI.at[s, c, way],
            send_sem=halo_send.at[s, c, way], recv_sem=halo_recv.at[s, c, way],
            device_id=(up if way == 0 else down, me), device_id_type=MESH,
        )

    def velocities(c):
        consts = C[c]
        aa, bb, cc, ss = (jnp.broadcast_to(consts[:, i:i + 1], (TILE, BLK)) for i in range(4))

        def one(j, carry):
            here = SM[j]
            speed = bb * jnp.tanh(aa * here[0:1])
            VX[c, j] = speed * cc + here[1:2]
            VY[c, j] = speed * ss + here[2:3]
            return carry

        lax.fori_loop(0, SLOTS, one, 0, unroll=8)

    def fluxes(s, c, par):
        if s == 0:
            velocities(c)
        wait_for(A.at[s, c, pl.ds(0, MEM - 1)], out_recv.at[s, c])

        def one(i, carry):
            for sl in range(2):
                j = 2 * i + sl
                g = A[s, c, i, sl].astype(F32)
                vx, vy = VX[c, j], VY[c, j]
                px, py = vx * g, vy * g
                east = jnp.where(vx > 0.0, px, 0.0)
                west = east - px
                north = jnp.where(vy > 0.0, py, 0.0)
                south = north - py
                from_west = pltpu.roll(east, 1, 1)
                from_east = pltpu.roll(west, BLK - 1, 1)
                inner = jnp.where(first_lane, 0.0, from_west) + jnp.where(last_lane, 0.0, from_east)
                NET[par, j] = inner - ((east + west) + (north + south))
                EDGE[par, j] = jnp.where(first_lane, from_west, from_east)
                FN[par, j] = north.astype(BF16)
                FS[par, j] = south.astype(BF16)
            return carry

        lax.fori_loop(0, MEM, one, 0, unroll=4)

        def edge(p, carry):
            HO[s, c, 0, p] = FN[par, TBS[0, 64 + p]]
            HO[s, c, 1, p] = FS[par, TBS[0, 16 + p]]
            return carry

        lax.fori_loop(0, MEM, edge, 0, unroll=4)
        halo_copy(s, c, 0).start()
        halo_copy(s, c, 1).start()

    def changes(s, c, par):
        halo_copy(s, c, 0).wait_recv()
        halo_copy(s, c, 1).wait_recv()
        FN[par, HALO:HALO + MEM] = HI[s, c, 0]
        FS[par, HALO:HALO + MEM] = HI[s, c, 1]

        def one(i, carry):
            for sl in range(2):
                j = 2 * i + sl
                sides = jnp.where(last_lane, EDGE[par, NB[1, j]], 0.0)
                sides = jnp.where(first_lane, EDGE[par, NB[0, j]], sides)
                lines = FN[par, NB[2, j]].astype(F32) + FS[par, NB[3, j]].astype(F32)
                R[s, c, i, sl] = (NET[par, j] + sides + lines).astype(BF16)
            return carry

        lax.fori_loop(0, MEM, one, 0, unroll=4)
        tile = 16 * c + me

        def send(o, carry):
            dst = peer(o)
            pltpu.make_async_remote_copy(
                src_ref=R.at[s, c, dst], dst_ref=D.at[s, tile],
                send_sem=ret_send.at[s, c], recv_sem=ret_recv.at[s, c],
                device_id=(band, dst), device_id_type=MESH,
            ).start()
            return carry

        lax.fori_loop(1, MEM, send, 0)
        D[s, tile] = R[s, c, me]

    def gather(s, r0, tiles, sums):
        def one(i, carry):
            rows = pl.ds(pl.multiple_of(r0 + i * TILE, TILE), TILE)
            new = []
            for sl in range(2):
                cols = slice(sl * BLK, (sl + 1) * BLK)
                x = S[rows, cols] + D[s, r0 // TILE + i, sl].astype(F32)
                S[rows, cols] = x
                LOW[rows, cols] = x.astype(BF16)
                new.append(carry[sl] + x * x)
            return tuple(new)

        return lax.fori_loop(0, tiles, one, sums, unroll=min(tiles, 4))

    def multiply(k0, depth, add):
        low = LOW[pl.ds(k0, depth), :]

        def one(i, carry):
            rows = pl.ds(pl.multiple_of(i * 432, 16), 432)
            for mix, total in ((M1, F1), (M2, F2)):
                got = jnp.dot(mix[rows, pl.ds(k0, depth)], low, preferred_element_type=F32)
                total[rows, :] = total[rows, :] + got if add else got
            return carry

        lax.fori_loop(0, 3, one, 0)

    def update(s, r0, tiles, spread):
        def one(i, carry):
            rows = pl.ds(pl.multiple_of(r0 + i * TILE, TILE), TILE)
            for sl in range(2):
                cols = slice(sl * BLK, (sl + 1) * BLK)
                scale = 1.0 + (WRB[rows, :] * OW[1:2, cols] - DSB[rows, :] * spread[sl])
                gated = 0.25 * F1[rows, cols] * (1.0 + jnp.tanh(0.5 * F2[rows, cols]))
                x = OW[0:1, cols] * (S[rows, cols] * scale + gated)
                if s == 0:
                    S[rows, cols] = x
                    G[1, r0 // TILE + i, sl] = x.astype(BF16)
                else:
                    out[rows, cols] = x
            return carry

        lax.fori_loop(0, tiles, one, 0, unroll=min(tiles, 4))

    start = jnp.where(me == HOT, -1, 0)
    for s in range(STEPS):
        def stage(i, carry, s=s):
            @pl.when(i < CHUNKS)
            def _():
                fluxes(s, jnp.where(i < 0, EXTRA, i), (i + 2) % 2)

            @pl.when(i > start)
            def _():
                changes(s, jnp.where(i < 1, EXTRA, i - 1), (i + 1) % 2)

            return carry

        lax.fori_loop(start, CHUNKS + 1, stage, 0)

        if s == 0:
            for one in mix_loads:
                one.wait()

        @pl.when(me != HOT)
        def _():
            wait_for(D.at[s, 80], ret_recv.at[s, EXTRA])

        zero = jnp.zeros((TILE, BLK), F32)
        sums = gather(s, 1280, 1, (zero, zero))
        multiply(1280, 16, False)

        def collect(t, sums, s=s):
            wait_for(D.at[s, pl.ds(16 * t, MEM - 1)], ret_recv.at[s, t])
            k0 = pl.multiple_of(t * 256, 256)
            sums = gather(s, k0, 16, sums)
            multiply(k0, 256, True)
            return sums

        sums = lax.fori_loop(0, CHUNKS, collect, sums)
        spread = [
            0.5 * jnp.sqrt(jnp.sum(one, axis=0, keepdims=True) * (1.0 / K) + 1e-06) for one in sums
        ]
        update(s, 1280, 1, spread)
        if s == 0:
            send_out(1, EXTRA)

        def finish(t, carry, s=s, spread=spread):
            update(s, pl.multiple_of(t * 256, 256), 16, spread)
            if s == 0:
                send_out(1, t)
            return carry

        lax.fori_loop(0, CHUNKS, finish, 0)

    wait_for(IDS.at[pl.ds(0, MEM - 1)], id_send)
    wait_for(META.at[pl.ds(0, MEM - 1)], meta_send)
    for s in range(STEPS):
        wait_for(G.at[s, pl.ds(0, 75)], out_send.at[s, 0])

        @pl.when(me != HOT)
        def _():
            wait_for(G.at[s, 80], out_send.at[s, 1])

        @pl.when(me == HOT)
        def _():
            wait_for(R.at[s, EXTRA, pl.ds(0, MEM - 1)], ret_send.at[s, EXTRA])
            for way in range(2):
                halo_copy(s, EXTRA, way).wait_send()
        for t in range(CHUNKS):
            wait_for(R.at[s, t, pl.ds(0, MEM - 1)], ret_send.at[s, t])
            for way in range(2):
                halo_copy(s, t, way).wait_send()


def on_device(action, block_list, land_sea, ice, depth, cur_x, cur_y, wind, wind_rate, dissipation, mix1, mix2):
    hbm = pl.BlockSpec(memory_space=pltpu.HBM)
    dma = pltpu.SemaphoreType.DMA
    tile = (TILE, BLK)

    def pinned(x):
        return pltpu.with_memory_space_constraint(x, pltpu.HBM)

    wet_part = pl.pallas_call(
        kernel,
        out_shape=pltpu.VMEM((K, 256), F32),
        in_specs=[hbm] * 13,
        out_specs=pl.BlockSpec(memory_space=pltpu.VMEM),
        scratch_shapes=[
            pltpu.SMEM((4,), jnp.int32),
            pltpu.VMEM((4, BLK), jnp.int32),
            pltpu.VMEM((4, BLK), jnp.int32),
            pltpu.VMEM((4, BLK), F32),
            pltpu.VMEM((4, BLK), F32),
            pltpu.VMEM((4, BLK), F32),
            pltpu.VMEM((4, BLK), F32),
            pltpu.VMEM((K,), F32),
            pltpu.VMEM((K,), F32),
            pltpu.VMEM((K, 256), F32),
            pltpu.VMEM((K, K), BF16),
            pltpu.VMEM((K, K), BF16),
            pltpu.VMEM((K, 256), BF16),
            pltpu.VMEM((K, 256), F32),
            pltpu.VMEM((K, 256), F32),
            pltpu.VMEM((STEPS, TILES, 2) + tile, BF16),
            pltpu.VMEM((STEPS, 6, MEM, 2) + tile, BF16),
            pltpu.VMEM((STEPS, 6, MEM, 2) + tile, BF16),
            pltpu.VMEM((STEPS, TILES, 2) + tile, BF16),
            pltpu.VMEM((STEPS, 6, 2, MEM) + tile, BF16),
            pltpu.VMEM((STEPS, 6, 2, MEM) + tile, BF16),
            pltpu.VMEM((2, SLOTS) + tile, F32),
            pltpu.VMEM((2, SLOTS + 1) + tile, F32),
            pltpu.VMEM((2, FIELD) + tile, BF16),
            pltpu.VMEM((2, FIELD) + tile, BF16),
            pltpu.VMEM((6, SLOTS) + tile, F32),
            pltpu.VMEM((6, SLOTS) + tile, F32),
            pltpu.VMEM((SLOTS, 8, BLK), F32),
            pltpu.VMEM((16, BLK), F32),
            pltpu.VMEM((MEM, 16, BLK), F32),
            pltpu.VMEM((8, BLK), jnp.int32),
            pltpu.VMEM((MEM, 8, BLK), jnp.int32),
            pltpu.VMEM((8, BLK), jnp.int32),
            pltpu.SMEM((8, BLK), jnp.int32),
            pltpu.SMEM((4, SLOTS), jnp.int32),
            pltpu.VMEM((6,) + tile, F32),
            pltpu.VMEM((K, BLK), F32),
            pltpu.VMEM((K, BLK), F32),
            pltpu.VMEM((8, 256), F32),
            dma((9,)), dma((6,)), dma((2,)), dma((6,)), dma, dma, dma, dma, dma,
            dma((STEPS, 2)), dma((STEPS, 6)), dma((STEPS, 6, 2)), dma((STEPS, 6, 2)),
            dma((STEPS, 6)), dma((STEPS, 6)),
        ],
        compiler_params=pltpu.CompilerParams(
            collective_id=0, has_side_effects=True, vmem_limit_bytes=48 * 1024 * 1024
        ),
        cost_estimate=pl.CostEstimate(flops=7 * 10**9, bytes_accessed=10**7, transcendentals=10**6),
    )(
        *(
            pinned(x)
            for x in (
                block_list, land_sea, ice, depth, cur_x, cur_y, wind, wind_rate, dissipation,
                jnp.asarray(component_table()), action, mix1, mix2,
            )
        ),
    )
    return jnp.concatenate([wet_part, jnp.zeros((K, action.shape[1] - 256), F32)], axis=1)


def solution(mesh):
    col = P(None, ("band", "grp"))
    flat = P(("band", "grp"))
    grid = P("band", "grp")
    return jax.shard_map(
        on_device,
        mesh=mesh,
        in_specs=(col, flat, grid, grid, grid, grid, grid, grid, P(), P(), P(), P()),
        out_specs=col,
        check_vma=False,
    )
```

time: 80.7 us -> 67.5 us (0.84)
  local copies, waits for them, and re-layouts: 10.8 us -> 1.87 us
  Pallas kernels: 69.4 us -> 65.5 us
    unnamed x18 -> x0, local copies, waits for them, and re-layouts: 7.58 us -> none
    pallas_call x1, Pallas kernels: 69.4 us -> 65.5 us  [on_device(): pl.pallas_call(kernel, out_shape=pltpu.VMEM((K, 256), F32), in_specs=[hbm...]
    reshape x2 -> x0, local copies, waits for them, and re-layouts: 1.4 us -> none  [the longest x1 0.7 us: on_device(): wind_rate.reshape(1, K)]
where the time goes in v1:
time: 67.5 us; the launch traced here: 67.4 us
  Pallas kernels  65.5 us (97%)
  local copies, waits for them, and re-layouts  1.87 us (3%)
    pallas_call x1, Pallas kernels, on_device(): pl.pallas_call(kernel, out_shape=pltpu.VMEM((K, 256), F32), in_specs=[hbm...  65.5 us
    concatenate x1, local copies, waits for them, and re-layouts, on_device(): jnp.concatenate([wet_part, jnp.zeros((K, action.shape[1] - 256), F32)], a...  1.87 us

profile of v1, /device:TPU:0, one launch (start us, length us, event | category | flops | bytes accessed | tf_op | source)
XLA Modules:
  0.0 67.4 jit_solution(2340215533499088379)
XLA Ops:
  0.0 65.5 %shard_map.127 = f32[1296,256]{1,0:T(8,128)S(1)} custom-call(s32[4]{0:T(128)} %bl_in.1, s32[4,128]{1,0:T(4,128)} %land_in.1, s32[4,128]{1,0:T(4,128)} %ice_in.1, f32[4,128]{1,0:T(4,128)} %depth_in.1, f32[4,128]{1,0:T(4,128)} %cur_x_in.1, f32[4,128]{1,0:T(4,128)} %cur_y_in.1, f32[4,128]{1,0:T(4,128)} %wind_in.1, f32[1296]{0:T(1024)} %wr_in.1, f32[1296]{0:T(1024)} %dis_in.1, ...), custom_call_target="tpu_custom_call" | custom-call | flops 7000000000 | bytes 10000000 | tf_op jit(solution)/shard_map/pallas_call | solution.py:463
  65.5 1.9 %concatenate.3 = f32[1296,512]{1,0:T(8,128)} pad(f32[1296,256]{1,0:T(8,128)S(1)} %shard_map.127, f32[]{:T(128)} %constant.1.clone.1), padding=0_0x0_256 | pad | bytes 3981316 | tf_op jit(solution)/shard_map/concatenate | solution.py:525

commit v2 on v1

--- a/solution.py
+++ b/solution.py
@@ -21,6 +21,9 @@
 CHUNKS = 5
 EXTRA = 5
 HOT = 0
+LAG = 3
+BUFS = LAG + 1
+ORDER = [(d // 4, d % 4) for d in range(1, 16)]
 ZERO = 32
 HALO = 33
 FIELD = 49
@@ -52,11 +55,15 @@
 ):
     band = lax.axis_index("band")
     me = lax.axis_index("grp")
-    mx, my = me // 4, me % 4
-    up, down = (band + 1) % BANDS, (band + BANDS - 1) % BANDS
-
-    def peer(o):
-        return ((mx + o // 4) % 4) * 4 + (my + o % 4) % 4
+    up, down = lax.rem(band + 1, BANDS), lax.rem(band + BANDS - 1, BANDS)
+
+    mx, my = lax.div(me, 4), lax.rem(me, 4)
+    line_of = [4 * lax.rem(mx + d, 4) for d in range(4)]
+    place_of = [lax.rem(my + d, 4) for d in range(4)]
+
+    def each_peer(act):
+        for dx, dy in ORDER:
+            act(line_of[dx] + place_of[dy])
 
     def rows_of(t):
         return (1280, 16) if t == EXTRA else (256 * t, 256)
@@ -91,11 +98,10 @@
 
     barrier = pltpu.get_barrier_semaphore()
 
-    def greet(o, carry):
-        pl.semaphore_signal(barrier, inc=1, device_id=(band, peer(o)), device_id_type=MESH)
-        return carry
-
-    lax.fori_loop(1, MEM, greet, 0)
+    def greet(dst):
+        pl.semaphore_signal(barrier, inc=1, device_id=(band, dst), device_id_type=MESH)
+
+    each_peer(greet)
     pl.semaphore_signal(barrier, inc=1, device_id=(up, me), device_id_type=MESH)
     pl.semaphore_signal(barrier, inc=1, device_id=(down, me), device_id_type=MESH)
 
@@ -112,13 +118,12 @@
     META[me] = MT[...]
     IDS[me] = IDT[...]
     for ref in (EDGE, FN, FS):
-        for par in range(2):
+        for par in range(BUFS):
             ref[par, ZERO] = jnp.zeros((TILE, BLK), ref.dtype)
 
     pl.semaphore_wait(barrier, MEM + 1)
 
-    def send_meta(o, carry):
-        dst = peer(o)
+    def send_meta(dst):
         pltpu.make_async_remote_copy(
             src_ref=IDT, dst_ref=IDS.at[me], send_sem=id_send, recv_sem=id_recv,
             device_id=(band, dst), device_id_type=MESH,
@@ -127,9 +132,8 @@
             src_ref=MT, dst_ref=META.at[me], send_sem=meta_send, recv_sem=meta_recv,
             device_id=(band, dst), device_id_type=MESH,
         ).start()
-        return carry
-
-    lax.fori_loop(1, MEM, send_meta, 0)
+
+    each_peer(send_meta)
 
     def send_out(s, t):
         if t is EXTRA:
@@ -146,16 +150,14 @@
                 A[s, EXTRA, HOT] = G[s, 80]
             return
 
-        def one(o, carry):
-            dst = peer(o)
+        def one(dst):
             pltpu.make_async_remote_copy(
                 src_ref=G.at[s, 16 * t + dst], dst_ref=A.at[s, t, me],
                 send_sem=out_send.at[s, 0], recv_sem=out_recv.at[s, t],
                 device_id=(band, dst), device_id_type=MESH,
             ).start()
-            return carry
-
-        lax.fori_loop(1, MEM, one, 0)
+
+        each_peer(one)
         A[s, t, me] = G[s, 16 * t + me]
 
     for t in order:
@@ -168,26 +170,27 @@
                 G[0, r0 // TILE + i, sl] = S[rows, sl * BLK:(sl + 1) * BLK].astype(BF16)
             return carry
 
-        lax.fori_loop(0, n // TILE, pack, 0)
+        lax.fori_loop(0, n // TILE, pack, 0, unroll=min(n // TILE, 4))
         send_out(0, t)
 
-    for one in small_loads[7:]:
-        one.wait()
-
-    def columns(i, carry):
-        part = pl.ds(pl.multiple_of(i * BLK, BLK), BLK)
-        diag = lax.broadcasted_iota(jnp.int32, (BLK, BLK), 0) == lax.broadcasted_iota(jnp.int32, (BLK, BLK), 1)
+    def rate_columns():
+        for one in small_loads[7:]:
+            one.wait()
+
+        def columns(i, carry):
+            part = pl.ds(pl.multiple_of(i * BLK, BLK), BLK)
+            diag = lax.broadcasted_iota(jnp.int32, (BLK, BLK), 0) == lax.broadcasted_iota(jnp.int32, (BLK, BLK), 1)
+            for src, dst in ((wr, WRB), (dis, DSB)):
+                col = jnp.sum(jnp.where(diag, src[part].reshape(1, BLK), 0.0), axis=1, keepdims=True)
+                dst[part, :] = jnp.broadcast_to(col, (BLK, BLK))
+            return carry
+
+        lax.fori_loop(0, K // BLK, columns, 0)
+        rest = K % BLK
+        diag = lax.broadcasted_iota(jnp.int32, (rest, rest), 0) == lax.broadcasted_iota(jnp.int32, (rest, rest), 1)
         for src, dst in ((wr, WRB), (dis, DSB)):
-            col = jnp.sum(jnp.where(diag, src[part].reshape(1, BLK), 0.0), axis=1, keepdims=True)
-            dst[part, :] = jnp.broadcast_to(col, (BLK, BLK))
-        return carry
-
-    lax.fori_loop(0, K // BLK, columns, 0)
-    rest = K % BLK
-    diag = lax.broadcasted_iota(jnp.int32, (rest, rest), 0) == lax.broadcasted_iota(jnp.int32, (rest, rest), 1)
-    for src, dst in ((wr, WRB), (dis, DSB)):
-        col = jnp.sum(jnp.where(diag, src[K - rest:K].reshape(1, rest), 0.0), axis=1, keepdims=True)
-        dst[K - rest:K, :] = jnp.broadcast_to(col, (rest, BLK))
+            col = jnp.sum(jnp.where(diag, src[K - rest:K].reshape(1, rest), 0.0), axis=1, keepdims=True)
+            dst[K - rest:K, :] = jnp.broadcast_to(col, (rest, BLK))
 
     def wait_for(ref, sem):
         pltpu.make_async_copy(ref, ref, sem).wait()
@@ -214,20 +217,21 @@
 
     def neighbours(j, carry):
         q = TBS[1, j]
-        line, place = (q // 16) * 16 + 16, q % 16
-        NB[0, j] = TBS[0, line + (place + 15) % 16]
-        NB[1, j] = TBS[0, line + (place + 1) % 16]
+        place = lax.rem(q, 16)
+        line = q - place + 16
+        NB[0, j] = TBS[0, line + lax.rem(place + 15, 16)]
+        NB[1, j] = TBS[0, line + lax.rem(place + 1, 16)]
         NB[2, j] = TBS[0, q]
         NB[3, j] = TBS[0, q + 32]
         return carry
 
-    lax.fori_loop(0, SLOTS, neighbours, 0)
+    lax.fori_loop(0, SLOTS, neighbours, 0, unroll=8)
 
     wait_for(META.at[pl.ds(0, MEM - 1)], meta_recv)
 
     def at_block(q):
-        found = META[q % 16]
-        r = q // 16
+        found = META[lax.rem(q, 16)]
+        r = lax.div(q, 16)
         pick = []
         for layer in range(4):
             got = found[4 * layer:4 * layer + 1]
@@ -243,7 +247,7 @@
         SM[j, 2:3] = wy
         return carry
 
-    lax.fori_loop(0, SLOTS, place_meta, 0)
+    lax.fori_loop(0, SLOTS, place_meta, 0, unroll=8)
     for sl in range(2):
         wd, _, _, wn = at_block(bl[sl])
         OW[0:1, sl * BLK:(sl + 1) * BLK] = jnp.where(wd > 0.0, 1.0, 0.0)
@@ -327,16 +331,14 @@
         lax.fori_loop(0, MEM, one, 0, unroll=4)
         tile = 16 * c + me
 
-        def send(o, carry):
-            dst = peer(o)
+        def send(dst):
             pltpu.make_async_remote_copy(
                 src_ref=R.at[s, c, dst], dst_ref=D.at[s, tile],
                 send_sem=ret_send.at[s, c], recv_sem=ret_recv.at[s, c],
                 device_id=(band, dst), device_id_type=MESH,
             ).start()
-            return carry
-
-        lax.fori_loop(1, MEM, send, 0)
+
+        each_peer(send)
         D[s, tile] = R[s, c, me]
 
     def gather(s, r0, tiles, sums):
@@ -387,17 +389,18 @@
         def stage(i, carry, s=s):
             @pl.when(i < CHUNKS)
             def _():
-                fluxes(s, jnp.where(i < 0, EXTRA, i), (i + 2) % 2)
-
-            @pl.when(i > start)
+                fluxes(s, jnp.where(i < 0, EXTRA, i), lax.rem(i + BUFS, BUFS))
+
+            @pl.when(i > start + LAG - 1)
             def _():
-                changes(s, jnp.where(i < 1, EXTRA, i - 1), (i + 1) % 2)
-
-            return carry
-
-        lax.fori_loop(start, CHUNKS + 1, stage, 0)
+                changes(s, jnp.where(i < LAG, EXTRA, i - LAG), lax.rem(i + BUFS - LAG, BUFS))
+
+            return carry
+
+        lax.fori_loop(start, CHUNKS + LAG, stage, 0)
 
         if s == 0:
+            rate_columns()
             for one in mix_loads:
                 one.wait()
 
@@ -487,10 +490,10 @@
             pltpu.VMEM((STEPS, TILES, 2) + tile, BF16),
             pltpu.VMEM((STEPS, 6, 2, MEM) + tile, BF16),
             pltpu.VMEM((STEPS, 6, 2, MEM) + tile, BF16),
-            pltpu.VMEM((2, SLOTS) + tile, F32),
-            pltpu.VMEM((2, SLOTS + 1) + tile, F32),
-            pltpu.VMEM((2, FIELD) + tile, BF16),
-            pltpu.VMEM((2, FIELD) + tile, BF16),
+            pltpu.VMEM((BUFS, SLOTS) + tile, F32),
+            pltpu.VMEM((BUFS, SLOTS + 1) + tile, F32),
+            pltpu.VMEM((BUFS, FIELD) + tile, BF16),
+            pltpu.VMEM((BUFS, FIELD) + tile, BF16),
             pltpu.VMEM((6, SLOTS) + tile, F32),
             pltpu.VMEM((6, SLOTS) + tile, F32),
             pltpu.VMEM((SLOTS, 8, BLK), F32),

time: 67.5 us -> 59.3 us (0.88)
  Pallas kernels: 65.5 us -> 57 us
    pallas_call x1, Pallas kernels: 65.5 us -> 57 us  [on_device(): pl.pallas_call(kernel, out_shape=pltpu.VMEM((K, 256), F32), in_specs=[hbm...]
where the time goes in v2:
time: 59.3 us; the launch traced here: 58.9 us
  Pallas kernels  57 us (96%)
  local copies, waits for them, and re-layouts  1.87 us (3%)
    pallas_call x1, Pallas kernels, on_device(): pl.pallas_call(kernel, out_shape=pltpu.VMEM((K, 256), F32), in_specs=[hbm...  57 us
    concatenate x1, local copies, waits for them, and re-layouts, on_device(): jnp.concatenate([wet_part, jnp.zeros((K, action.shape[1] - 256), F32)], a...  1.87 us

profile of v2, /device:TPU:0, one launch (start us, length us, event | category | flops | bytes accessed | tf_op | source)
XLA Modules:
  0.0 58.9 jit_solution(4422291466861352614)
XLA Ops:
  0.0 57.0 %shard_map.127 = f32[1296,256]{1,0:T(8,128)S(1)} custom-call(s32[4]{0:T(128)} %bl_in.1, s32[4,128]{1,0:T(4,128)} %land_in.1, s32[4,128]{1,0:T(4,128)} %ice_in.1, f32[4,128]{1,0:T(4,128)} %depth_in.1, f32[4,128]{1,0:T(4,128)} %cur_x_in.1, f32[4,128]{1,0:T(4,128)} %cur_y_in.1, f32[4,128]{1,0:T(4,128)} %wind_in.1, f32[1296]{0:T(1024)} %wr_in.1, f32[1296]{0:T(1024)} %dis_in.1, ...), custom_call_target="tpu_custom_call" | custom-call | flops 7000000000 | bytes 10000000 | tf_op jit(solution)/shard_map/pallas_call | solution.py:466
  57.0 1.9 %concatenate.3 = f32[1296,512]{1,0:T(8,128)} pad(f32[1296,256]{1,0:T(8,128)S(1)} %shard_map.127, f32[]{:T(128)} %constant.1.clone.1), padding=0_0x0_256 | pad | bytes 3981316 | tf_op jit(solution)/shard_map/concatenate | solution.py:528

commit v3 on v2

--- a/solution.py
+++ b/solution.py
@@ -23,7 +23,7 @@
 HOT = 0
 LAG = 3
 BUFS = LAG + 1
-ORDER = [(d // 4, d % 4) for d in range(1, 16)]
+ORDER = sorted([(d // 4, d % 4) for d in range(1, 16)], key=lambda d: -min(d[0], 4 - d[0]) - min(d[1], 4 - d[1]))
 ZERO = 32
 HALO = 33
 FIELD = 49
@@ -44,12 +44,47 @@
     return table.reshape(TILES, TILE, BLK)
 
 
+def sourced(S, F1, F2, WRB, DSB, OW, rows, sl):
+    cols = slice(sl * BLK, (sl + 1) * BLK)
+    scale = 1.0 + (WRB[rows, :] * OW[1:2, cols] - DSB[rows, :] * OW[2:3, cols])
+    gated = F1[rows, cols] * (0.25 + 0.25 * jnp.tanh(0.5 * F2[rows, cols]))
+    return OW[0:1, cols] * (S[rows, cols] * scale + gated)
+
+
+def last_kernel(S, F1, F2, WRB, DSB, OW, out, made, zeros, made_sem, zero_sem):
+    zeros[...] = jnp.zeros_like(zeros)
+    part = K // 9
+    for n in range(9):
+        pltpu.make_async_copy(
+            zeros, out.at[pl.ds(part * n, part), pl.ds(256, 256)], zero_sem.at[n]
+        ).start()
+
+    def copy_of(n):
+        rows = pl.ds(part * n, part)
+        return pltpu.make_async_copy(made.at[rows], out.at[rows, pl.ds(0, 256)], made_sem.at[n])
+
+    for n in range(9):
+        def one(i, carry, n=n):
+            rows = pl.ds(pl.multiple_of(part * n + i * TILE, TILE), TILE)
+            for sl in range(2):
+                made[rows, sl * BLK:(sl + 1) * BLK] = sourced(S, F1, F2, WRB, DSB, OW, rows, sl)
+            return carry
+
+        lax.fori_loop(0, part // TILE, one, 0, unroll=3)
+        copy_of(n).start()
+    for n in range(9):
+        pltpu.make_async_copy(
+            zeros, out.at[pl.ds(part * n, part), pl.ds(256, 256)], zero_sem.at[n]
+        ).wait()
+        copy_of(n).wait()
+
+
 def kernel(
     bl_in, land_in, ice_in, depth_in, cur_x_in, cur_y_in, wind_in, wr_in, dis_in, cst, action, mix1, mix2,
-    out,
+    S, F1, F2, WRB, DSB, OW,
     bl, land, ice, depth, cur_x, cur_y, wind, wr, dis,
-    S, M1, M2, LOW, F1, F2, G, A, R, D, HO, HI, NET, EDGE, FN, FS, VX, VY, SM,
-    MT, META, IDT, IDS, TBL, TBS, NB, C, WRB, DSB, OW,
+    M1, M2, LOW, G, A, R, D, HO, HI, NET, EDGE, FN, FS, VX, VY, SM,
+    MT, META, IDT, IDS, TBL, TBS, NB, C,
     small_sem, act_sem, mix_sem, cst_sem, tbl_sem, meta_send, meta_recv, id_send, id_recv,
     out_send, out_recv, halo_send, halo_recv, ret_send, ret_recv,
 ):
@@ -302,7 +337,7 @@
                 FS[par, j] = south.astype(BF16)
             return carry
 
-        lax.fori_loop(0, MEM, one, 0, unroll=4)
+        lax.fori_loop(0, MEM, one, 0, unroll=8)
 
         def edge(p, carry):
             HO[s, c, 0, p] = FN[par, TBS[0, 64 + p]]
@@ -328,7 +363,7 @@
                 R[s, c, i, sl] = (NET[par, j] + sides + lines).astype(BF16)
             return carry
 
-        lax.fori_loop(0, MEM, one, 0, unroll=4)
+        lax.fori_loop(0, MEM, one, 0, unroll=8)
         tile = 16 * c + me
 
         def send(dst):
@@ -367,19 +402,13 @@
 
         lax.fori_loop(0, 3, one, 0)
 
-    def update(s, r0, tiles, spread):
+    def update(r0, tiles):
         def one(i, carry):
             rows = pl.ds(pl.multiple_of(r0 + i * TILE, TILE), TILE)
             for sl in range(2):
-                cols = slice(sl * BLK, (sl + 1) * BLK)
-                scale = 1.0 + (WRB[rows, :] * OW[1:2, cols] - DSB[rows, :] * spread[sl])
-                gated = 0.25 * F1[rows, cols] * (1.0 + jnp.tanh(0.5 * F2[rows, cols]))
-                x = OW[0:1, cols] * (S[rows, cols] * scale + gated)
-                if s == 0:
-                    S[rows, cols] = x
-                    G[1, r0 // TILE + i, sl] = x.astype(BF16)
-                else:
-                    out[rows, cols] = x
+                x = sourced(S, F1, F2, WRB, DSB, OW, rows, sl)
+                S[rows, sl * BLK:(sl + 1) * BLK] = x
+                G[1, r0 // TILE + i, sl] = x.astype(BF16)
             return carry
 
         lax.fori_loop(0, tiles, one, 0, unroll=min(tiles, 4))
@@ -420,20 +449,20 @@
             return sums
 
         sums = lax.fori_loop(0, CHUNKS, collect, sums)
-        spread = [
-            0.5 * jnp.sqrt(jnp.sum(one, axis=0, keepdims=True) * (1.0 / K) + 1e-06) for one in sums
-        ]
-        update(s, 1280, 1, spread)
+        for sl in range(2):
+            mean = jnp.sum(sums[sl], axis=0, keepdims=True) * (1.0 / K)
+            OW[2:3, sl * BLK:(sl + 1) * BLK] = 0.5 * jnp.sqrt(mean + 1e-06)
+
         if s == 0:
+            update(1280, 1)
             send_out(1, EXTRA)
 
-        def finish(t, carry, s=s, spread=spread):
-            update(s, pl.multiple_of(t * 256, 256), 16, spread)
-            if s == 0:
+            def finish(t, carry):
+                update(pl.multiple_of(t * 256, 256), 16)
                 send_out(1, t)
-            return carry
-
-        lax.fori_loop(0, CHUNKS, finish, 0)
+                return carry
+
+            lax.fori_loop(0, CHUNKS, finish, 0)
 
     wait_for(IDS.at[pl.ds(0, MEM - 1)], id_send)
     wait_for(META.at[pl.ds(0, MEM - 1)], meta_send)
@@ -463,11 +492,18 @@
     def pinned(x):
         return pltpu.with_memory_space_constraint(x, pltpu.HBM)
 
-    wet_part = pl.pallas_call(
+    state = pl.pallas_call(
         kernel,
-        out_shape=pltpu.VMEM((K, 256), F32),
+        out_shape=[
+            pltpu.VMEM((K, 256), F32),
+            pltpu.VMEM((K, 256), F32),
+            pltpu.VMEM((K, 256), F32),
+            pltpu.VMEM((K, BLK), F32),
+            pltpu.VMEM((K, BLK), F32),
+            pltpu.VMEM((8, 256), F32),
+        ],
         in_specs=[hbm] * 13,
-        out_specs=pl.BlockSpec(memory_space=pltpu.VMEM),
+        out_specs=[pl.BlockSpec(memory_space=pltpu.VMEM)] * 6,
         scratch_shapes=[
             pltpu.SMEM((4,), jnp.int32),
             pltpu.VMEM((4, BLK), jnp.int32),
@@ -478,12 +514,9 @@
             pltpu.VMEM((4, BLK), F32),
             pltpu.VMEM((K,), F32),
             pltpu.VMEM((K,), F32),
-            pltpu.VMEM((K, 256), F32),
             pltpu.VMEM((K, K), BF16),
             pltpu.VMEM((K, K), BF16),
             pltpu.VMEM((K, 256), BF16),
-            pltpu.VMEM((K, 256), F32),
-            pltpu.VMEM((K, 256), F32),
             pltpu.VMEM((STEPS, TILES, 2) + tile, BF16),
             pltpu.VMEM((STEPS, 6, MEM, 2) + tile, BF16),
             pltpu.VMEM((STEPS, 6, MEM, 2) + tile, BF16),
@@ -505,9 +538,6 @@
             pltpu.SMEM((8, BLK), jnp.int32),
             pltpu.SMEM((4, SLOTS), jnp.int32),
             pltpu.VMEM((6,) + tile, F32),
-            pltpu.VMEM((K, BLK), F32),
-            pltpu.VMEM((K, BLK), F32),
-            pltpu.VMEM((8, 256), F32),
             dma((9,)), dma((6,)), dma((2,)), dma((6,)), dma, dma, dma, dma, dma,
             dma((STEPS, 2)), dma((STEPS, 6)), dma((STEPS, 6, 2)), dma((STEPS, 6, 2)),
             dma((STEPS, 6)), dma((STEPS, 6)),
@@ -525,7 +555,18 @@
             )
         ),
     )
-    return jnp.concatenate([wet_part, jnp.zeros((K, action.shape[1] - 256), F32)], axis=1)
+    return pl.pallas_call(
+        last_kernel,
+        out_shape=jax.ShapeDtypeStruct(action.shape, F32),
+        in_specs=[pl.BlockSpec(memory_space=pltpu.VMEM)] * 6,
+        out_specs=hbm,
+        scratch_shapes=[
+            pltpu.VMEM((K, 256), F32),
+            pltpu.VMEM((K // 9, 256), F32),
+            dma((9,)), dma((9,)),
+        ],
+        compiler_params=pltpu.CompilerParams(vmem_limit_bytes=8 * 1024 * 1024),
+    )(*state)
 
 
 def solution(mesh):

time: 59.3 us -> 57 us (0.961)
  local copies, waits for them, and re-layouts: 1.87 us -> 0 us
  Pallas kernels: 57 us -> 56.4 us
    concatenate x1 -> x0, local copies, waits for them, and re-layouts: 1.87 us -> none  [on_device(): jnp.concatenate([wet_part, jnp.zeros((K, action.shape[1] - 256), F32)], a...]
    pallas_call x1 -> x2, Pallas kernels: 57 us -> 56.4 us  [the longest x1 54.7 us: on_device(): pl.pallas_call(kernel, out_shape=[pltpu.VMEM((K, 256), F32), pltpu.VMEM((...]
where the time goes in v3:
time: 57 us; the launch traced here: 56.4 us
  Pallas kernels  56.4 us (99%)
    pallas_call x1, Pallas kernels, on_device(): pl.pallas_call(kernel, out_shape=[pltpu.VMEM((K, 256), F32), pltpu.VMEM((...  54.7 us
    pallas_call x1, Pallas kernels, on_device(): pl.pallas_call(last_kernel, out_shape=jax.ShapeDtypeStruct(action.shape,...  1.66 us

profile of v3, /device:TPU:0, one launch (start us, length us, event | category | flops | bytes accessed | tf_op | source)
XLA Modules:
  0.0 56.4 jit_solution(8934377226962660704)
XLA Ops:
  0.0 54.7 %shard_map.127 = (f32[1296,256]{1,0:T(8,128)S(1)}, f32[1296,256]{1,0:T(8,128)S(1)}, f32[1296,256]{1,0:T(8,128)S(1)}, f32[1296,128]{1,0:T(8,128)S(1)}, f32[1296,128]{1,0:T(8,128)S(1)}, /*index=5*/f32[8,256]{1,0:T(8,128)S(1)}) custom-call(s32[4]{0:T(128)} %bl_in.1, s32[4,128]{1,0:T(4,128)} %land_in.1, s32[4,128]{1,0:T(4,128)} %ice_in.1, f32[4,128]{1,0:T(4,128)} %depth_in.1, ...), custom_call_target="tpu_custom_call" | custom-call | flops 7000000000 | bytes 10000000 | tf_op jit(solution)/shard_map/pallas_call | solution.py:495
  54.8 1.7 %shard_map.128 = f32[1296,512]{1,0:T(8,128)} custom-call(f32[1296,256]{1,0:T(8,128)S(1)} %get-tuple-element.11.S, f32[1296,256]{1,0:T(8,128)S(1)} %get-tuple-element.12.F1, f32[1296,256]{1,0:T(8,128)S(1)} %get-tuple-element.13.F2, f32[1296,128]{1,0:T(8,128)S(1)} %get-tuple-element.14.WRB, f32[1296,128]{1,0:T(8,128)S(1)} %get-tuple-element.15.DSB, ...), custom_call_target="tpu_custom_call" | custom-call | tf_op jit(solution)/shard_map/pallas_call | solution.py:558

commit v4 on v3

--- a/solution.py
+++ b/solution.py
@@ -84,8 +84,8 @@
     S, F1, F2, WRB, DSB, OW,
     bl, land, ice, depth, cur_x, cur_y, wind, wr, dis,
     M1, M2, LOW, G, A, R, D, HO, HI, NET, EDGE, FN, FS, VX, VY, SM,
-    MT, META, IDT, IDS, TBL, TBS, NB, C,
-    small_sem, act_sem, mix_sem, cst_sem, tbl_sem, meta_send, meta_recv, id_send, id_recv,
+    MT, META, WND, IDT, IDS, TBL, TBS, NB, C,
+    small_sem, act_sem, mix_sem, cst_sem, tbl_sem, meta_send, meta_recv, id_send, id_recv, wind_send, wind_recv,
     out_send, out_recv, halo_send, halo_recv, ret_send, ret_recv,
 ):
     band = lax.axis_index("band")
@@ -143,15 +143,14 @@
     for one in small_loads[:7]:
         one.wait()
     wet = land[...].astype(F32) * (1.0 - ice[...].astype(F32))
-    MT[0:4] = wet * depth[...]
-    MT[4:8] = wet * cur_x[...]
-    MT[8:12] = wet * cur_y[...]
-    MT[12:16] = wind[...]
-    IDT[...] = jnp.zeros_like(IDT)
+    MT[0] = wet * depth[...]
+    MT[1] = wet * cur_x[...]
+    MT[2] = wet * cur_y[...]
     IDT[0:1] = jnp.full((1, BLK), bl[0], jnp.int32)
     IDT[1:2] = jnp.full((1, BLK), bl[1], jnp.int32)
     META[me] = MT[...]
     IDS[me] = IDT[...]
+    WND[me] = wind[...]
     for ref in (EDGE, FN, FS):
         for par in range(BUFS):
             ref[par, ZERO] = jnp.zeros((TILE, BLK), ref.dtype)
@@ -195,11 +194,14 @@
         each_peer(one)
         A[s, t, me] = G[s, 16 * t + me]
 
-    for t in order:
+    def wait_for(ref, sem):
+        pltpu.make_async_copy(ref, ref, sem).wait()
+
+    def first_out(t):
         r0, n = rows_of(t)
         loads[t].wait()
 
-        def pack(i, carry, r0=r0):
+        def pack(i, carry):
             rows = pl.ds(pl.multiple_of(r0 + i * TILE, TILE), TILE)
             for sl in range(2):
                 G[0, r0 // TILE + i, sl] = S[rows, sl * BLK:(sl + 1) * BLK].astype(BF16)
@@ -208,27 +210,8 @@
         lax.fori_loop(0, n // TILE, pack, 0, unroll=min(n // TILE, 4))
         send_out(0, t)
 
-    def rate_columns():
-        for one in small_loads[7:]:
-            one.wait()
-
-        def columns(i, carry):
-            part = pl.ds(pl.multiple_of(i * BLK, BLK), BLK)
-            diag = lax.broadcasted_iota(jnp.int32, (BLK, BLK), 0) == lax.broadcasted_iota(jnp.int32, (BLK, BLK), 1)
-            for src, dst in ((wr, WRB), (dis, DSB)):
-                col = jnp.sum(jnp.where(diag, src[part].reshape(1, BLK), 0.0), axis=1, keepdims=True)
-                dst[part, :] = jnp.broadcast_to(col, (BLK, BLK))
-            return carry
-
-        lax.fori_loop(0, K // BLK, columns, 0)
-        rest = K % BLK
-        diag = lax.broadcasted_iota(jnp.int32, (rest, rest), 0) == lax.broadcasted_iota(jnp.int32, (rest, rest), 1)
-        for src, dst in ((wr, WRB), (dis, DSB)):
-            col = jnp.sum(jnp.where(diag, src[K - rest:K].reshape(1, rest), 0.0), axis=1, keepdims=True)
-            dst[K - rest:K, :] = jnp.broadcast_to(col, (rest, BLK))
-
-    def wait_for(ref, sem):
-        pltpu.make_async_copy(ref, ref, sem).wait()
+    for t in order[:3]:
+        first_out(t)
 
     wait_for(IDS.at[pl.ds(0, MEM - 1)], id_recv)
     lane = lax.broadcasted_iota(jnp.int32, (1, BLK), 1)
@@ -248,6 +231,35 @@
     TBL[1:2] = named
     to_smem = pltpu.make_async_copy(TBL, TBS, tbl_sem)
     to_smem.start()
+    for t in order[3:]:
+        first_out(t)
+
+    def send_wind(dst):
+        pltpu.make_async_remote_copy(
+            src_ref=wind, dst_ref=WND.at[me], send_sem=wind_send, recv_sem=wind_recv,
+            device_id=(band, dst), device_id_type=MESH,
+        ).start()
+
+    each_peer(send_wind)
+    def rate_columns():
+        for one in small_loads[7:]:
+            one.wait()
+
+        def columns(i, carry):
+            part = pl.ds(pl.multiple_of(i * BLK, BLK), BLK)
+            diag = lax.broadcasted_iota(jnp.int32, (BLK, BLK), 0) == lax.broadcasted_iota(jnp.int32, (BLK, BLK), 1)
+            for src, dst in ((wr, WRB), (dis, DSB)):
+                col = jnp.sum(jnp.where(diag, src[part].reshape(1, BLK), 0.0), axis=1, keepdims=True)
+                dst[part, :] = jnp.broadcast_to(col, (BLK, BLK))
+            return carry
+
+        lax.fori_loop(0, K // BLK, columns, 0)
+        rest = K % BLK
+        diag = lax.broadcasted_iota(jnp.int32, (rest, rest), 0) == lax.broadcasted_iota(jnp.int32, (rest, rest), 1)
+        for src, dst in ((wr, WRB), (dis, DSB)):
+            col = jnp.sum(jnp.where(diag, src[K - rest:K].reshape(1, rest), 0.0), axis=1, keepdims=True)
+            dst[K - rest:K, :] = jnp.broadcast_to(col, (rest, BLK))
+
     to_smem.wait()
 
     def neighbours(j, carry):
@@ -264,29 +276,20 @@
 
     wait_for(META.at[pl.ds(0, MEM - 1)], meta_recv)
 
-    def at_block(q):
-        found = META[lax.rem(q, 16)]
-        r = lax.div(q, 16)
-        pick = []
-        for layer in range(4):
-            got = found[4 * layer:4 * layer + 1]
-            for k in range(1, 4):
-                got = jnp.where(r == k, found[4 * layer + k:4 * layer + k + 1], got)
-            pick.append(got)
-        return pick
+    def line_at(found, r):
+        got = found[0:1]
+        for k in range(1, 4):
+            got = jnp.where(r == k, found[k:k + 1], got)
+        return got
 
     def place_meta(j, carry):
-        wd, wx, wy, _ = at_block(TBS[1, j])
-        SM[j, 0:1] = wd
-        SM[j, 1:2] = wx
-        SM[j, 2:3] = wy
+        q = TBS[1, j]
+        place, r = lax.rem(q, 16), lax.div(q, 16)
+        for layer in range(3):
+            SM[j, layer:layer + 1] = line_at(META[place, layer], r)
         return carry
 
     lax.fori_loop(0, SLOTS, place_meta, 0, unroll=8)
-    for sl in range(2):
-        wd, _, _, wn = at_block(bl[sl])
-        OW[0:1, sl * BLK:(sl + 1) * BLK] = jnp.where(wd > 0.0, 1.0, 0.0)
-        OW[1:2, sl * BLK:(sl + 1) * BLK] = 0.5 * wn
     for one in table_loads:
         one.wait()
 
@@ -390,17 +393,20 @@
 
         return lax.fori_loop(0, tiles, one, sums, unroll=min(tiles, 4))
 
-    def multiply(k0, depth, add):
+    def multiply(k0, depth, add, r0=0, height=432, parts=3):
         low = LOW[pl.ds(k0, depth), :]
 
         def one(i, carry):
-            rows = pl.ds(pl.multiple_of(i * 432, 16), 432)
+            rows = pl.ds(pl.multiple_of(r0 + i * height, 16), height)
             for mix, total in ((M1, F1), (M2, F2)):
                 got = jnp.dot(mix[rows, pl.ds(k0, depth)], low, preferred_element_type=F32)
                 total[rows, :] = total[rows, :] + got if add else got
             return carry
 
-        lax.fori_loop(0, 3, one, 0)
+        if parts == 1:
+            one(0, 0)
+        else:
+            lax.fori_loop(0, parts, one, 0)
 
     def update(r0, tiles):
         def one(i, carry):
@@ -430,6 +436,12 @@
 
         if s == 0:
             rate_columns()
+            wait_for(WND.at[pl.ds(0, MEM - 1)], wind_recv)
+            for sl in range(2):
+                place, r = lax.rem(bl[sl], 16), lax.div(bl[sl], 16)
+                cols = slice(sl * BLK, (sl + 1) * BLK)
+                OW[0:1, cols] = jnp.where(line_at(META[place, 0], r) > 0.0, 1.0, 0.0)
+                OW[1:2, cols] = 0.5 * line_at(WND[place], r)
             for one in mix_loads:
                 one.wait()
 
@@ -445,20 +457,27 @@
             wait_for(D.at[s, pl.ds(16 * t, MEM - 1)], ret_recv.at[s, t])
             k0 = pl.multiple_of(t * 256, 256)
             sums = gather(s, k0, 16, sums)
-            multiply(k0, 256, True)
+            if s == 1 or t is not CHUNKS - 1:
+                multiply(k0, 256, True)
             return sums
 
-        sums = lax.fori_loop(0, CHUNKS, collect, sums)
+        if s == 0:
+            sums = collect(CHUNKS - 1, lax.fori_loop(0, CHUNKS - 1, collect, sums))
+        else:
+            sums = lax.fori_loop(0, CHUNKS, collect, sums)
         for sl in range(2):
             mean = jnp.sum(sums[sl], axis=0, keepdims=True) * (1.0 / K)
             OW[2:3, sl * BLK:(sl + 1) * BLK] = 0.5 * jnp.sqrt(mean + 1e-06)
 
         if s == 0:
+            multiply(1024, 256, True, 1280, 16, 1)
             update(1280, 1)
             send_out(1, EXTRA)
 
             def finish(t, carry):
-                update(pl.multiple_of(t * 256, 256), 16)
+                r0 = pl.multiple_of(t * 256, 256)
+                multiply(1024, 256, True, r0, 256, 1)
+                update(r0, 16)
                 send_out(1, t)
                 return carry
 
@@ -466,6 +485,7 @@
 
     wait_for(IDS.at[pl.ds(0, MEM - 1)], id_send)
     wait_for(META.at[pl.ds(0, MEM - 1)], meta_send)
+    wait_for(WND.at[pl.ds(0, MEM - 1)], wind_send)
     for s in range(STEPS):
         wait_for(G.at[s, pl.ds(0, 75)], out_send.at[s, 0])
 
@@ -530,15 +550,16 @@
             pltpu.VMEM((6, SLOTS) + tile, F32),
             pltpu.VMEM((6, SLOTS) + tile, F32),
             pltpu.VMEM((SLOTS, 8, BLK), F32),
-            pltpu.VMEM((16, BLK), F32),
-            pltpu.VMEM((MEM, 16, BLK), F32),
-            pltpu.VMEM((8, BLK), jnp.int32),
-            pltpu.VMEM((MEM, 8, BLK), jnp.int32),
+            pltpu.VMEM((3, 4, BLK), F32),
+            pltpu.VMEM((MEM, 3, 4, BLK), F32),
+            pltpu.VMEM((MEM, 4, BLK), F32),
+            pltpu.VMEM((2, BLK), jnp.int32),
+            pltpu.VMEM((MEM, 2, BLK), jnp.int32),
             pltpu.VMEM((8, BLK), jnp.int32),
             pltpu.SMEM((8, BLK), jnp.int32),
             pltpu.SMEM((4, SLOTS), jnp.int32),
             pltpu.VMEM((6,) + tile, F32),
-            dma((9,)), dma((6,)), dma((2,)), dma((6,)), dma, dma, dma, dma, dma,
+            dma((9,)), dma((6,)), dma((2,)), dma((6,)), dma, dma, dma, dma, dma, dma, dma,
             dma((STEPS, 2)), dma((STEPS, 6)), dma((STEPS, 6, 2)), dma((STEPS, 6, 2)),
             dma((STEPS, 6)), dma((STEPS, 6)),
         ],

time: 57 us -> 55.2 us (0.968)
  Pallas kernels: 56.4 us -> 55.1 us
    pallas_call x1, Pallas kernels: 54.7 us -> 53.4 us  [on_device(): pl.pallas_call(kernel, out_shape=[pltpu.VMEM((K, 256), F32), pltpu.VMEM((...]
where the time goes in v4:
time: 55.2 us; the launch traced here: 55.1 us
  Pallas kernels  55.1 us (100%)
    pallas_call x1, Pallas kernels, on_device(): pl.pallas_call(kernel, out_shape=[pltpu.VMEM((K, 256), F32), pltpu.VMEM((...  53.4 us
    pallas_call x1, Pallas kernels, on_device(): pl.pallas_call(last_kernel, out_shape=jax.ShapeDtypeStruct(action.shape,...  1.66 us

profile of v4, /device:TPU:0, one launch (start us, length us, event | category | flops | bytes accessed | tf_op | source)
XLA Modules:
  0.0 55.1 jit_solution(9131389331419744389)
XLA Ops:
  0.0 53.4 %shard_map.127 = (f32[1296,256]{1,0:T(8,128)S(1)}, f32[1296,256]{1,0:T(8,128)S(1)}, f32[1296,256]{1,0:T(8,128)S(1)}, f32[1296,128]{1,0:T(8,128)S(1)}, f32[1296,128]{1,0:T(8,128)S(1)}, /*index=5*/f32[8,256]{1,0:T(8,128)S(1)}) custom-call(s32[4]{0:T(128)} %bl_in.1, s32[4,128]{1,0:T(4,128)} %land_in.1, s32[4,128]{1,0:T(4,128)} %ice_in.1, f32[4,128]{1,0:T(4,128)} %depth_in.1, ...), custom_call_target="tpu_custom_call" | custom-call | flops 7000000000 | bytes 10000000 | tf_op jit(solution)/shard_map/pallas_call | solution.py:515
  53.4 1.7 %shard_map.128 = f32[1296,512]{1,0:T(8,128)} custom-call(f32[1296,256]{1,0:T(8,128)S(1)} %get-tuple-element.11.S, f32[1296,256]{1,0:T(8,128)S(1)} %get-tuple-element.12.F1, f32[1296,256]{1,0:T(8,128)S(1)} %get-tuple-element.13.F2, f32[1296,128]{1,0:T(8,128)S(1)} %get-tuple-element.14.WRB, f32[1296,128]{1,0:T(8,128)S(1)} %get-tuple-element.15.DSB, ...), custom_call_target="tpu_custom_call" | custom-call | tf_op jit(solution)/shard_map/pallas_call | solution.py:579

commit v5 on v4

--- a/solution.py
+++ b/solution.py
@@ -274,6 +274,7 @@
 
     lax.fori_loop(0, SLOTS, neighbours, 0, unroll=8)
 
+    rate_columns()
     wait_for(META.at[pl.ds(0, MEM - 1)], meta_recv)
 
     def line_at(found, r):
@@ -393,7 +394,7 @@
 
         return lax.fori_loop(0, tiles, one, sums, unroll=min(tiles, 4))
 
-    def multiply(k0, depth, add, r0=0, height=432, parts=3):
+    def multiply(k0, depth, add, r0=0, height=1296, parts=1):
         low = LOW[pl.ds(k0, depth), :]
 
         def one(i, carry):
@@ -435,7 +436,6 @@
         lax.fori_loop(start, CHUNKS + LAG, stage, 0)
 
         if s == 0:
-            rate_columns()
             wait_for(WND.at[pl.ds(0, MEM - 1)], wind_recv)
             for sl in range(2):
                 place, r = lax.rem(bl[sl], 16), lax.div(bl[sl], 16)

time: 55.2 us -> 53.8 us (0.975)
  Pallas kernels: 55.1 us -> 53.7 us
    pallas_call x1, Pallas kernels: 53.4 us -> 52 us  [on_device(): pl.pallas_call(kernel, out_shape=[pltpu.VMEM((K, 256), F32), pltpu.VMEM((...]
where the time goes in v5:
time: 53.8 us; the launch traced here: 53.7 us
  Pallas kernels  53.7 us (100%)
    pallas_call x1, Pallas kernels, on_device(): pl.pallas_call(kernel, out_shape=[pltpu.VMEM((K, 256), F32), pltpu.VMEM((...  52 us
    pallas_call x1, Pallas kernels, on_device(): pl.pallas_call(last_kernel, out_shape=jax.ShapeDtypeStruct(action.shape,...  1.66 us

profile of v5, /device:TPU:0, one launch (start us, length us, event | category | flops | bytes accessed | tf_op | source)
XLA Modules:
  0.0 53.7 jit_solution(8952387741154118310)
XLA Ops:
  0.0 52.0 %shard_map.127 = (f32[1296,256]{1,0:T(8,128)S(1)}, f32[1296,256]{1,0:T(8,128)S(1)}, f32[1296,256]{1,0:T(8,128)S(1)}, f32[1296,128]{1,0:T(8,128)S(1)}, f32[1296,128]{1,0:T(8,128)S(1)}, /*index=5*/f32[8,256]{1,0:T(8,128)S(1)}) custom-call(s32[4]{0:T(128)} %bl_in.1, s32[4,128]{1,0:T(4,128)} %land_in.1, s32[4,128]{1,0:T(4,128)} %ice_in.1, f32[4,128]{1,0:T(4,128)} %depth_in.1, ...), custom_call_target="tpu_custom_call" | custom-call | flops 7000000000 | bytes 10000000 | tf_op jit(solution)/shard_map/pallas_call | solution.py:515
  52.0 1.7 %shard_map.128 = f32[1296,512]{1,0:T(8,128)} custom-call(f32[1296,256]{1,0:T(8,128)S(1)} %get-tuple-element.11.S, f32[1296,256]{1,0:T(8,128)S(1)} %get-tuple-element.12.F1, f32[1296,256]{1,0:T(8,128)S(1)} %get-tuple-element.13.F2, f32[1296,128]{1,0:T(8,128)S(1)} %get-tuple-element.14.WRB, f32[1296,128]{1,0:T(8,128)S(1)} %get-tuple-element.15.DSB, ...), custom_call_target="tpu_custom_call" | custom-call | tf_op jit(solution)/shard_map/pallas_call | solution.py:579

commit v6 on v5

--- a/solution.py
+++ b/solution.py
@@ -20,7 +20,6 @@
 STEPS = 2
 CHUNKS = 5
 EXTRA = 5
-HOT = 0
 LAG = 3
 BUFS = LAG + 1
 ORDER = sorted([(d // 4, d % 4) for d in range(1, 16)], key=lambda d: -min(d[0], 4 - d[0]) - min(d[1], 4 - d[1]))
@@ -92,6 +91,8 @@
     me = lax.axis_index("grp")
     up, down = lax.rem(band + 1, BANDS), lax.rem(band + BANDS - 1, BANDS)
 
+    hot = 10 * lax.rem(band, 2)
+    hot_beside = 10 - hot
     mx, my = lax.div(me, 4), lax.rem(me, 4)
     line_of = [4 * lax.rem(mx + d, 4) for d in range(4)]
     place_of = [lax.rem(my + d, 4) for d in range(4)]
@@ -140,6 +141,11 @@
     pl.semaphore_signal(barrier, inc=1, device_id=(up, me), device_id_type=MESH)
     pl.semaphore_signal(barrier, inc=1, device_id=(down, me), device_id_type=MESH)
 
+    @pl.when(me == hot)
+    def _():
+        for side in (up, down):
+            pl.semaphore_signal(barrier, inc=1, device_id=(side, hot_beside), device_id_type=MESH)
+
     for one in small_loads[:7]:
         one.wait()
     wet = land[...].astype(F32) * (1.0 - ice[...].astype(F32))
@@ -155,7 +161,7 @@
         for par in range(BUFS):
             ref[par, ZERO] = jnp.zeros((TILE, BLK), ref.dtype)
 
-    pl.semaphore_wait(barrier, MEM + 1)
+    pl.semaphore_wait(barrier, MEM + 1 + jnp.where(me == hot, 2, 0))
 
     def send_meta(dst):
         pltpu.make_async_remote_copy(
@@ -171,17 +177,17 @@
 
     def send_out(s, t):
         if t is EXTRA:
-            @pl.when(me != HOT)
+            @pl.when(me != hot)
             def _():
                 pltpu.make_async_remote_copy(
                     src_ref=G.at[s, 80], dst_ref=A.at[s, EXTRA, me],
                     send_sem=out_send.at[s, 1], recv_sem=out_recv.at[s, EXTRA],
-                    device_id=(band, HOT), device_id_type=MESH,
+                    device_id=(band, hot), device_id_type=MESH,
                 ).start()
 
-            @pl.when(me == HOT)
+            @pl.when(me == hot)
             def _():
-                A[s, EXTRA, HOT] = G[s, 80]
+                A[s, EXTRA, me] = G[s, 80]
             return
 
         def one(dst):
@@ -301,7 +307,7 @@
         return pltpu.make_async_remote_copy(
             src_ref=HO.at[s, c, way], dst_ref=HI.at[s, c, way],
             send_sem=halo_send.at[s, c, way], recv_sem=halo_recv.at[s, c, way],
-            device_id=(up if way == 0 else down, me), device_id_type=MESH,
+            device_id=(up if way == 0 else down, jnp.where(c == EXTRA, hot_beside, me)), device_id_type=MESH,
         )
 
     def velocities(c):
@@ -368,7 +374,7 @@
             return carry
 
         lax.fori_loop(0, MEM, one, 0, unroll=8)
-        tile = 16 * c + me
+        tile = jnp.where(c == EXTRA, 80, 16 * c + me)
 
         def send(dst):
             pltpu.make_async_remote_copy(
@@ -420,7 +426,7 @@
 
         lax.fori_loop(0, tiles, one, 0, unroll=min(tiles, 4))
 
-    start = jnp.where(me == HOT, -1, 0)
+    start = jnp.where(me == hot, -1, 0)
     for s in range(STEPS):
         def stage(i, carry, s=s):
             @pl.when(i < CHUNKS)
@@ -445,7 +451,7 @@
             for one in mix_loads:
                 one.wait()
 
-        @pl.when(me != HOT)
+        @pl.when(me != hot)
         def _():
             wait_for(D.at[s, 80], ret_recv.at[s, EXTRA])
 
@@ -489,11 +495,11 @@
     for s in range(STEPS):
         wait_for(G.at[s, pl.ds(0, 75)], out_send.at[s, 0])
 
-        @pl.when(me != HOT)
+        @pl.when(me != hot)
         def _():
             wait_for(G.at[s, 80], out_send.at[s, 1])
 
-        @pl.when(me == HOT)
+        @pl.when(me == hot)
         def _():
             wait_for(R.at[s, EXTRA, pl.ds(0, MEM - 1)], ret_send.at[s, EXTRA])
             for way in range(2):

time: 53.8 us -> 62.9 us (1.17)
  Pallas kernels: 53.7 us -> 62.8 us
    pallas_call x1, Pallas kernels: 52 us -> 61.1 us  [on_device(): pl.pallas_call(kernel, out_shape=[pltpu.VMEM((K, 256), F32), pltpu.VMEM((...]
where the time goes in v6:
time: 62.9 us; the launch traced here: 62.8 us
  Pallas kernels  62.8 us (100%)
    pallas_call x1, Pallas kernels, on_device(): pl.pallas_call(kernel, out_shape=[pltpu.VMEM((K, 256), F32), pltpu.VMEM((...  61.1 us
    pallas_call x1, Pallas kernels, on_device(): pl.pallas_call(last_kernel, out_shape=jax.ShapeDtypeStruct(action.shape,...  1.66 us

profile of v6, /device:TPU:0, one launch (start us, length us, event | category | flops | bytes accessed | tf_op | source)
XLA Modules:
  0.0 62.8 jit_solution(18431249868425484351)
XLA Ops:
  0.0 61.1 %shard_map.127 = (f32[1296,256]{1,0:T(8,128)S(1)}, f32[1296,256]{1,0:T(8,128)S(1)}, f32[1296,256]{1,0:T(8,128)S(1)}, f32[1296,128]{1,0:T(8,128)S(1)}, f32[1296,128]{1,0:T(8,128)S(1)}, /*index=5*/f32[8,256]{1,0:T(8,128)S(1)}) custom-call(s32[4]{0:T(128)} %bl_in.1, s32[4,128]{1,0:T(4,128)} %land_in.1, s32[4,128]{1,0:T(4,128)} %ice_in.1, f32[4,128]{1,0:T(4,128)} %depth_in.1, ...), custom_call_target="tpu_custom_call" | custom-call | flops 7000000000 | bytes 10000000 | tf_op jit(solution)/shard_map/pallas_call | solution.py:521
  61.1 1.7 %shard_map.128 = f32[1296,512]{1,0:T(8,128)} custom-call(f32[1296,256]{1,0:T(8,128)S(1)} %get-tuple-element.11.S, f32[1296,256]{1,0:T(8,128)S(1)} %get-tuple-element.12.F1, f32[1296,256]{1,0:T(8,128)S(1)} %get-tuple-element.13.F2, f32[1296,128]{1,0:T(8,128)S(1)} %get-tuple-element.14.WRB, f32[1296,128]{1,0:T(8,128)S(1)} %get-tuple-element.15.DSB, ...), custom_call_target="tpu_custom_call" | custom-call | tf_op jit(solution)/shard_map/pallas_call | solution.py:585
